TPU v7x, 256 devices: a whole 4x4x8 slice. The times are simulated.
256 devices in a mesh: ri: 32 (over x_hi, z, core), occ: 8 (over x_lo, y).
Axes of the slice: x: 4 (x_hi: 2, x_lo: 2; x = x_hi * 2 + x_lo), y: 4, z: 8, core: 2. Of those that a mesh axis runs over, the one named last changes fastest.
Arguments:
- three_index: bfloat16 [32768, 32, 256], P('ri', 'occ'), may hold values from -0.4375 to 0.4375
- polar_prev: float32 [2048, 32768], P('occ', 'ri'), may hold values from -6 to 6
- states: bfloat16 [32768, 64, 256], P('ri', 'occ'), may hold values from -0.005859375 to 0.005859375
- mo_energy: float32 [1024], replicated, may hold values from -3 to -0.1
- vir_energy: float32 [256], replicated, may hold values from 0.1 to 3
- orbital_energy: float32 [256], replicated, may hold values from -3 to 3
- occ_index: int32 [32], P('occ'), may hold values from 0 to 1023
- state_index: int32 [64], P('occ'), may hold values from 0 to 1023
- slab_rows: int32 [2048], replicated, may hold values from 0 to 32767, as said below
Outputs:
- polar_panel: float32 [2048, 32768], P('occ', 'ri')
- sigma: float32 [64], P('occ')
Inputs may be any that keep to these rules, and one draw needn't show every extreme that they name: `slab_rows`: entry q lies among rows b * 1024 to (b + 1) * 1024 - 1 with b = (q mod 256) // 8; the 64 entries that lie in one such block are distinct and include the block's first and last row.
All inputs are finite; a program needn't handle non-finite values.
Results may differ from a plain program's by a relative error of at most 0.0017.
Values may be sent and summed in bfloat16 or wider, within the bound.
A program may use at most 128 MiB of HBM per device.

v0:
```python
import jax
import jax.numpy as jnp
from jax import lax
from jax.sharding import PartitionSpec as P


def lookup_energy(table, index):
    positions = jnp.arange(table.shape[0], dtype=jnp.int32)
    matches = index[:, None] == positions[None, :]
    return jnp.sum(jnp.where(matches, table[None, :], 0.0), axis=1)


def local(
    three_index,
    polar_prev,
    states,
    mo_energy,
    vir_energy,
    orbital_energy,
    occ_index,
    state_index,
    slab_rows,
):
    ri_count = lax.axis_size("ri")
    occ_count = lax.axis_size("occ")
    ri_pos = lax.axis_index("ri")
    p_dev = three_index.shape[0]
    col_block = polar_prev.shape[0]
    per_sub = col_block // ri_count
    ns_dev = states.shape[1]
    orbitals = states.shape[2]
    arranged = slab_rows.reshape(occ_count, ri_count, per_sub)
    own_rows = lax.dynamic_index_in_dim(arranged, ri_pos, axis=1, keepdims=False)
    local_rows = (own_rows - ri_pos * p_dev).reshape(occ_count * per_sub)
    occ_energy = lookup_energy(mo_energy, occ_index)
    energy_gap = vir_energy[None, :] - occ_energy[:, None]
    pair_weight = 4.0 * energy_gap / (energy_gap * energy_gap + 0.25)
    picked = three_index[local_rows]
    scaled = (picked.astype(jnp.float32) * pair_weight[None]).astype(jnp.bfloat16)
    regrouped = lax.all_to_all(scaled, "occ", split_axis=0, concat_axis=1, tiled=True)
    slab_cols = lax.all_gather(regrouped, "ri", axis=0, tiled=True)
    product = lax.dot_general(
        slab_cols,
        lax.all_gather(three_index, "occ", axis=1, tiled=True),
        (((1, 2), (1, 2)), ((), ())),
        preferred_element_type=jnp.float32,
    )
    polar_panel = polar_prev - product
    screened = polar_panel.astype(jnp.bfloat16)
    state_rows = states[local_rows]
    state_gathered = lax.all_gather(state_rows, "ri", axis=0, tiled=True)
    state_grid = state_gathered.reshape(ri_count, occ_count, per_sub, ns_dev * orbitals)
    portion = lax.all_gather(screened, "occ", axis=0, tiled=True)
    groups = portion.shape[0] // col_block
    panel_grid = portion.reshape(groups, ri_count, per_sub, p_dev)
    applied = jnp.einsum(
        "krsP,rksf->Pf", panel_grid, state_grid, preferred_element_type=jnp.float32
    )
    local_pairs = jnp.sum(states.reshape(p_dev, ns_dev * orbitals) * applied, axis=0).reshape(
        ns_dev, orbitals
    )
    pair_sum = lax.psum(local_pairs, "ri")
    state_energy = lookup_energy(mo_energy, state_index)
    difference = state_energy[:, None] - orbital_energy[None, :]
    factor = difference / (difference * difference + 0.25)
    sigma = jnp.sum(factor * pair_sum, axis=1)
    return (polar_panel, sigma)


def solution(mesh):
    in_specs = (
        P("ri", "occ", None),
        P("occ", "ri"),
        P("ri", "occ", None),
        P(),
        P(),
        P(),
        P("occ"),
        P("occ"),
        P(),
    )
    out_specs = (P("occ", "ri"), P("occ"))
    return jax.shard_map(local, mesh=mesh, in_specs=in_specs, out_specs=out_specs, check_vma=False)
```

profile of v0, /device:TPU:1, one launch (start us, length us, event | category | flops | bytes accessed | tf_op | source)
XLA Modules:
  0.0 528.8 jit_solution(651037955357805650)
XLA Ops:
  7.2 0.9 reshape.78
  8.1 0.1 sub.52
  8.2 2.3 gather_fusion
  10.5 0.9 select_reduce_fusion.1
  11.4 0.8 fusion.9
  12.2 0.1 multiply_convert_fusion
  12.2 11.2 %all_to_all.18 = bf16[64,4,256]{2,1,0:T(4,128)(2,1)S(1)} all-to-all(bf16[64,4,256]{2,1,0:T(4,128)(2,1)S(1)} %multiply_convert_fusion), channel_id=1, replica_groups=mesh['ri'=32,'occ'=8] {'occ'}, dimensions={0} | all-to-all | bytes 262144 | tf_op jit(solution)/shard_map/all_to_all | solution.py:40
  23.4 0.7 copy.21
  24.1 0.0 all-gather.8.cloned.1.call-start
  24.2 3.2 copy.22
  27.4 0.0 all-gather.12.cloned.1.call-start
  27.5 3.5 gather_fusion.1
  31.0 0.0 all-gather.10.cloned.1.call-start
  31.0 82.6 %all-gather.6.cloned.1.call-done = bf16[256,32,256]{2,0,1:T(8,128)(2,1)} async-done(((bf16[8,32,256]{2,0,1:T(8,128)(2,1)}), bf16[256,32,256]{2,0,1:T(8,128)(2,1)}) %all-gather.6.cloned.1.call-update) | async-done | bytes 4194320 | tf_op jit(solution)/shard_map/all_gather | solution.py:41
  113.7 171.3 %all-gather.8.cloned.1.call-done = bf16[1024,32,256]{2,0,1:T(8,128)(2,1)} async-done(((bf16[1024,4,256]{2,0,1:T(8,128)(2,1)}), bf16[1024,32,256]{2,0,1:T(8,128)(2,1)}) %all-gather.8.cloned.1.call-update) | async-done | bytes 16777232 | tf_op jit(solution)/shard_map/all_gather | solution.py:44
  284.9 12.8 %fusion.12 = (bf16[256,1024]{1,0:T(8,128)(2,1)}, f32[256,1024]{1,0:T(8,128)}) fusion(f32[256,1024]{1,0:T(8,128)S(1)} %copy-done.4, bf16[256,32,256]{2,0,1:T(8,128)(2,1)} %all-gather.6.cloned.1.call-done, bf16[1024,32,256]{2,0,1:T(8,128)(2,1)} %all-gather.8.cloned.1.call-done), kind=kOutput, calls=%fused_computation.26 | convolution fusion | flops 4295491584 | bytes 23592960 | tf_op jit(solution)/shard_map/dot_general | solution.py:42
  297.7 7.7 %copy.25 = f32[128,8,8,256]{3,1,2,0:T(8,128)} copy(bf16[128,8,8,256]{3,2,1,0:T(8,128)(2,1)} %bitcast.24) | data formatting | bytes 12582912
  305.4 0.7 select_reduce_fusion
  306.1 82.3 %all-gather.12.cloned.1.call-done = bf16[2048,8,256]{2,1,0:T(8,128)(2,1)} async-done(((bf16[64,8,256]{2,1,0:T(8,128)(2,1)}), bf16[2048,8,256]{2,1,0:T(8,128)(2,1)}) %all-gather.12.cloned.1.call-update) | async-done | bytes 8388624 | tf_op jit(solution)/shard_map/all_gather | solution.py:51
  388.5 13.5 %reshape.80 = bf16[32,8,8,2048]{3,2,1,0:T(8,128)(2,1)} reshape(bf16[2048,8,256]{2,1,0:T(8,128)(2,1)} %all-gather.12.cloned.1.call-done) | data formatting | bytes 16777216 | tf_op jit(solution)/shard_map/reshape | solution.py:52
  401.9 39.5 %all-gather.10.cloned.1.call-done = bf16[2048,1024]{1,0:T(8,128)(2,1)} async-done(((bf16[256,1024]{1,0:T(8,128)(2,1)}), bf16[2048,1024]{1,0:T(8,128)(2,1)}) %all-gather.10.cloned.1.call-update) | async-done | bytes 4194320 | tf_op jit(solution)/shard_map/all_gather | solution.py:53
  441.4 13.9 %fusion = f32[2048]{0:T(1024)S(1)} fusion(f32[1024,2048]{1,0:T(8,128)} %bitcast.23, bf16[8,32,8,1024]{3,2,1,0:T(8,128)(2,1)} %bitcast.27, bf16[32,8,8,2048]{3,2,1,0:T(8,128)(2,1)} %reshape.80), kind=kOutput, calls=%fused_computation.3 | convolution fusion | flops 8594126848 | bytes 20979712 | tf_op jit(solution)/shard_map/krsP,rksf->Pf/dot_general | solution.py:56
  455.3 66.2 %psum.7 = f32[8,256]{1,0:T(8,128)S(1)} all-reduce(f32[8,256]{1,0:T(8,128)S(1)} %reshape.81), channel_id=1, replica_groups=mesh['ri'=32,'occ'=8] {'ri'}, use_global_device_ids=true, to_apply=%region_3.4 | all-reduce | flops 2048 | bytes 16384 | tf_op jit(solution)/shard_map/psum | solution.py:62
  521.5 0.7 fusion.8
  (19 shorter events, 0.2 us)
Async XLA Ops:
  7.2 277.8 %copy-start.4 = (f32[256,1024]{1,0:T(8,128)S(1)}, f32[256,1024]{1,0:T(8,128)}, u32[]{:S(2)}) copy-start(f32[256,1024]{1,0:T(8,128)} %param.10) | copy-start | bytes 3145732
  7.2 106.5 %all-gather.6.cloned.1.call-start = ((), (), s32[]{:S(2)}) async-start(), calls=%async_computation.1 | async-start | bytes 4325376 | tf_op jit(solution)/shard_map/all_gather | solution.py:41
  24.1 260.8 %all-gather.8.cloned.1.call-start = ((), (), s32[]{:S(2)}) async-start(), calls=%async_computation.2 | async-start | bytes 18874368 | tf_op jit(solution)/shard_map/all_gather | solution.py:44
  27.4 361.1 %all-gather.12.cloned.1.call-start = ((), (), s32[]{:S(2)}) async-start(), calls=%async_computation.4 | async-start | bytes 8650752 | tf_op jit(solution)/shard_map/all_gather | solution.py:51
  31.0 410.4 %all-gather.10.cloned.1.call-start = ((), (), s32[]{:S(2)}) async-start(), calls=%async_computation.3 | async-start | bytes 4718592 | tf_op jit(solution)/shard_map/all_gather | solution.py:53
  297.7 7.7 %copy-start = (f32[1024]{0:T(1024)S(1)}, f32[1024]{0:T(1024)}, u32[]{:S(2)}) copy-start(f32[1024]{0:T(1024)} %param.12) | copy-start | bytes 12292
  297.7 7.7 %copy-start.3 = (s32[8]{0:T(128)S(1)}, s32[8]{0:T(128)}, u32[]{:S(2)}) copy-start(s32[8]{0:T(128)} %param.16) | copy-start | bytes 100
  441.4 80.1 %copy-start.1 = (f32[8]{0:T(128)S(1)}, f32[8]{0:T(128)}, u32[]{:S(2)}) copy-start(f32[8]{0:T(128)} %select_reduce_fusion) | copy-start | bytes 100
  441.4 80.1 %copy-start.2 = (f32[256]{0:T(256)S(1)}, f32[256]{0:T(256)}, u32[]{:S(2)}) copy-start(f32[256]{0:T(256)} %param.14) | copy-start | bytes 3076
Sparse Core Ops, SparseCore 0:
  24.2 89.3 all-gather.5
  115.4 169.4 all-gather.7
  287.7 100.6 all-gather.11
  390.1 51.2 all-gather.9
where the time goes:
time: 532 us; the launch traced here: 529 us
  waiting for transfers between devices  376 us (71%)
  blocking collectives  77.4 us (15%)
  local copies, waits for them, and re-layouts  31.8 us (6%)
  matrix products  26.6 us (5%)
  between operations  13.9 us (3%)
    all_gather x1, waiting for transfers between devices, local(): lax.all_gather(three_index, 'occ', axis=1, tiled=True)  171 us
    all_gather x1, waiting for transfers between devices, local(): slab_cols = lax.all_gather(regrouped, 'ri', axis=0, tiled=True)  82.6 us
    all_gather x1, waiting for transfers between devices, local(): state_gathered = lax.all_gather(state_rows, 'ri', axis=0, tiled=True)  82.3 us
    psum x1, blocking collectives, local(): pair_sum = lax.psum(local_pairs, 'ri')  66.2 us
    all_gather x1, waiting for transfers between devices, local(): portion = lax.all_gather(screened, 'occ', axis=0, tiled=True)  39.5 us
    dot_general x1, matrix products, local(): jnp.einsum('krsP,rksf->Pf', panel_grid, state_grid, preferred_element_typ...  13.9 us
    reshape x1, local copies, waits for them, and re-layouts, local(): state_gathered.reshape(ri_count, occ_count, per_sub, ns_dev * orbitals)  13.5 us
    dot_general x1, matrix products, local(): lax.dot_general(slab_cols, lax.all_gather(three_index, 'occ', axis=1, til...  12.8 us
  transfers between devices with their start and end apart: 4, of which 4 were waited for; matrix products, arithmetic and copies ran while one was open for 8% of the time, Pallas kernels for 0%

commit v1 on v0

v1 whole, which is shorter than its diff:
```python
import jax
import jax.numpy as jnp
from jax import lax
from jax.experimental import pallas as pl
from jax.experimental.pallas import tpu as pltpu
from jax.sharding import PartitionSpec as P

HI, Z, CORE, LO, YS = 2, 8, 2, 2, 4
CHUNKS = Z
LANE = 128
HALF = 16
Y_FIRST = 4

STAGES = 19
(
    RELAY, A_OPP, D_OWN, D_OPP, A_RING, A_RING2, D_RING, D_RING2, PART, SUM, PASS, PASS_Y, SUM_Y, PANEL,
    NEAR, FAR_R, FAR_L, PAIRS,
) = range(1, STAGES)
ORDER = (
    (A_RING, 1), (A_RING, 2), (A_OPP, 0), (PART, 0), (A_RING, 3), (A_RING, 4), (A_RING2, 1), (A_RING2, 2),
    (RELAY, 0), (PASS_Y, 0), (SUM_Y, 0), (SUM, 0), (PART, 1), (PART, 2), (A_RING2, 3), (D_OWN, 0),
    (A_RING2, 4), (A_RING, 5), (A_RING, 6), (PASS, 0), (PASS_Y, 1), (PANEL, 0), (PART, 3), (PASS_Y, 2),
    (PART, 4), (FAR_R, 0), (SUM_Y, 1), (A_RING2, 6), (SUM_Y, 2), (D_OPP, 0), (PASS_Y, 3), (A_RING2, 5),
    (A_RING, 7), (PASS_Y, 4), (SUM, 1), (NEAR, 0), (PART, 5), (D_RING, 2), (PART, 6), (SUM_Y, 3), (SUM_Y, 4),
    (SUM, 2), (A_RING2, 7), (D_RING, 1), (PASS, 1), (FAR_L, 0), (PART, 7), (PANEL, 1), (PASS_Y, 5), (PASS, 2),
    (D_RING2, 1), (SUM, 3), (PASS_Y, 6), (SUM, 4), (D_RING2, 2), (PANEL, 2), (D_RING, 4), (PAIRS, 0),
    (SUM_Y, 5), (D_RING, 3), (NEAR, 1), (FAR_R, 1), (PASS, 3), (SUM_Y, 6), (SUM, 5), (PASS, 4), (PASS_Y, 7),
    (FAR_R, 2), (SUM, 6), (PANEL, 3), (D_RING2, 3), (NEAR, 2), (SUM, 7), (PANEL, 4), (NEAR, 3), (D_RING2, 4),
    (PASS, 5), (FAR_L, 1), (NEAR, 4), (D_RING, 6), (SUM_Y, 7), (D_RING, 5), (PASS, 6), (PANEL, 5), (PASS, 7),
    (D_RING2, 6), (FAR_L, 2), (D_RING2, 5), (NEAR, 5), (PANEL, 6), (FAR_R, 3), (FAR_L, 3), (PANEL, 7),
    (FAR_R, 4), (NEAR, 6), (PAIRS, 1), (FAR_L, 4), (D_RING, 7), (D_RING2, 7), (NEAR, 7), (FAR_R, 5),
    (PAIRS, 2), (FAR_L, 5), (FAR_R, 6), (PAIRS, 3), (FAR_L, 6), (FAR_R, 7), (PAIRS, 4), (FAR_L, 7),
    (PAIRS, 5), (PAIRS, 6), (PAIRS, 7),
)

MESH = pl.DeviceIdType.MESH
F32 = jnp.float32
BF16 = jnp.bfloat16


def remote(src, dst, send_sem, recv_sem, target):
    return pltpu.make_async_remote_copy(
        src_ref=src, dst_ref=dst, send_sem=send_sem, recv_sem=recv_sem,
        device_id=target, device_id_type=MESH,
    )


def tile_scale(peak):
    peak = jnp.max(jnp.max(peak, axis=0, keepdims=True), axis=1, keepdims=True)
    return jnp.floor(jnp.log(jnp.maximum(peak, 1e-20) * 1.001) * 1.4426950408889634) + 1.0


def encode(blocks, message):
    peak = None
    for load in blocks:
        for lane in load.lanes:
            high = jnp.abs(load(lane))
            peak = high if peak is None else jnp.maximum(peak, high)
    exponent = tile_scale(peak)
    inverse = jnp.exp2(15.0 - exponent)
    at = 0
    for load in blocks:
        for lane in load.lanes:
            message[at] = jnp.round(load(lane) * inverse).astype(jnp.int32).astype(jnp.int16)
            at += 1
    message[at] = jnp.broadcast_to(exponent, (HALF, LANE)).astype(jnp.int32).astype(jnp.int16)


def unit(message, last):
    return jnp.exp2(message[last].astype(jnp.int32).astype(F32) - 15.0)


def decode(message, at, scale):
    return message[at].astype(jnp.int32).astype(F32) * scale


class Rows:
    def __init__(self, ref, block, first, lanes):
        self.ref, self.block, self.first, self.lanes = ref, block, first, lanes

    def __call__(self, lane):
        return self.ref[self.block, pl.ds(self.first, HALF), pl.ds(lane, LANE)]


def kernel(
    x_ref, s3_ref, prev_ref, vir_ref, orb_ref, mo_ref, occ_idx, state_idx, slab_rows,
    out_ref, sig_ref,
    cols, slab, part, x_out, x_in, y_out, y_in, m_out, m_in, n_out, n_in, p_out, p_in, w_out, w_in,
    scr, acc, sg_chip, sg_line, s_ref, wide, relayed,
    a_recv, a_sib, a_send, a_opp, d_recv, d_sib, d_send, d_opp,
    x_send, x_recv, y_send, y_recv, m_send, m_recv, n_send, n_recv, p_send, p_recv, w_send, w_recv,
    c_send, c_recv, g_send, g_recv, l_send, l_recv, r_send, r_recv,
):
    width = prev_ref.shape[1]
    x_lanes = range(0, width - Y_FIRST * LANE, LANE)
    y_lanes = range(width - Y_FIRST * LANE, width, LANE)
    x_tiles, y_tiles = len(x_lanes), len(y_lanes)
    ri, k = lax.axis_index("ri"), lax.axis_index("occ")
    core = lax.rem(ri, CORE)
    z = lax.rem(ri // CORE, Z)
    hi = ri // (CORE * Z)
    y = lax.rem(k, YS)
    lo = k // YS
    xo = 1 - lo

    def ri_at(h, zz, c):
        return (h * Z + zz) * CORE + c

    def occ_at(x, yy):
        return x * YS + yy

    up = (ri_at(hi, lax.rem(z + 1, Z), core), k)
    down = (ri_at(hi, lax.rem(z + Z - 1, Z), core), k)
    sibling = (ri_at(hi, z, 1 - core), k)
    opposite = (ri_at(1 - hi, z, core), k)
    across = (ri_at(1 - hi, z, 1 - core), k)
    partner = (ri, occ_at(xo, y))
    diagonal = (ri_at(1 - hi, z, core), occ_at(xo, y))
    y_next, y_last, y_far = lax.rem(y + 1, YS), lax.rem(y + YS - 1, YS), lax.rem(y + 2, YS)
    right, left = (ri, occ_at(lo, y_next)), (ri, occ_at(lo, y_last))
    line = [(ri_at(hi, lax.rem(z + s, Z), core), k) for s in range(1, Z)]

    barrier = pltpu.get_barrier_semaphore()
    friends = [sibling, opposite, across, partner, diagonal, right, left] + line
    for friend in friends:
        pl.semaphore_signal(barrier, inc=1, device_id=friend, device_id_type=MESH)

    per_sub = prev_ref.shape[0] // (HI * Z * CORE)
    picks = LO * YS * per_sub
    groups = []
    for kk in range(LO * YS):
        spot = lax.broadcasted_iota(jnp.int32, (per_sub, LANE), 0)
        rows = jnp.zeros((per_sub, LANE), jnp.int32)
        for s in range(per_sub):
            row = slab_rows[kk * prev_ref.shape[0] + ri * per_sub + s] - ri * x_ref.shape[0]
            rows = jnp.where(spot == s, row, rows)
        groups.append(rows)
    rows = jnp.concatenate(groups, axis=0)
    place = lax.broadcasted_iota(jnp.int32, (picks, LANE), 1)
    chosen = jnp.concatenate(
        [jnp.where(place + lane == rows, 1.0, 0.0) for lane in range(0, x_ref.shape[0], LANE)], axis=1
    ).astype(BF16)
    weights = []
    for i in range(occ_idx.shape[0]):
        gap = vir_ref[...] - mo_ref[occ_idx[i]]
        weights.append(4.0 * gap / (gap * gap + 0.25))
    weight = jnp.concatenate(weights, axis=1)
    picked = jnp.dot(chosen, x_ref[...], preferred_element_type=F32)
    cols[z, core, hi] = (picked * weight).astype(BF16)

    pl.semaphore_wait(barrier, len(friends))

    a_set = (cols, a_recv, a_sib, a_send, a_opp)
    d_set = (slab, d_recv, d_sib, d_send, d_opp)

    def to_opposite(group):
        buf, recv, sib, send, opp = group
        shard = buf.at[z, core, hi]
        return remote(shard, shard, opp.at[0], recv.at[z, hi], opposite)

    def to_line(group, zz, h, way):
        buf, recv, sib, send, opp = group
        shard = buf.at[zz, core, h]
        ahead = (ri_at(hi, lax.rem(z + jnp.where(way == 0, 1, Z - 1), Z), core), k)
        return remote(shard, shard, send.at[zz, h, way], recv.at[zz, h], ahead)

    def to_sibling(group, zz, h):
        buf, recv, sib, send, opp = group
        shard = buf.at[zz, core, h]
        return remote(shard, shard, send.at[zz, h, 2], sib.at[zz, h], sibling)

    def await_shard(group, zz, h):
        buf, recv, sib, send, opp = group
        shard = buf.at[zz, core, h]
        remote(shard, shard, send.at[zz, h, 0], recv.at[zz, h], up).wait_recv()

    def await_sibling(group, zz):
        buf, recv, sib, send, opp = group
        for h in range(HI):
            shard = buf.at[zz, 1 - core, h]
            remote(shard, shard, send.at[zz, h, 2], sib.at[zz, h], sibling).wait_recv()

    def ring(group, c, far, act, arrive):
        zz = chunk_z(c)
        h = 1 - hi if far else hi
        way = lax.rem(c + 1, 2)
        if arrive:
            await_shard(group, zz, h)

        @pl.when(jnp.logical_or(c < 5, jnp.logical_and(c < 7, way == far)))
        def _():
            act(to_line(group, zz, h, way))

        act(to_sibling(group, zz, h))

    def start(copy):
        copy.start()

    def finish(copy):
        copy.wait_send()

    def chunk_z(t):
        return lax.rem(z + jnp.where(lax.rem(t, 2) == 1, Z - (t + 1) // 2, t // 2), Z)

    def panel_part(t):
        zz = chunk_z(t)
        await_sibling(a_set, zz)
        shards = CORE * HI
        lhs = cols[zz].reshape(shards * picks, cols.shape[-1])
        step = 256
        for first in range(0, width, step):
            res = lax.dot_general(
                lhs, x_ref[pl.ds(first, step), :], (((1,), (1,)), ((), ())),
                preferred_element_type=F32,
            )
            for kk in range(LO * YS):
                for g in range(shards):
                    part[t * (LO * YS) + kk, pl.ds(g * 8, 8), pl.ds(first, step)] = res[
                        g * picks + kk * 8 : g * picks + kk * 8 + 8
                    ]
        for way in range(2):
            beside = (y_next, y_last)[way]
            blocks = [Rows(part, at(t, lx, y_far), way * HALF, y_lanes) for lx in range(LO)]
            blocks += [Rows(part, at(t, lx, beside), (1 - way) * HALF, y_lanes) for lx in range(LO)]
            encode(blocks, n_out.at[t, way])
            n_copy(t, way).start()
        blocks = []
        for yy in range(YS):
            for first in (0, HALF):
                blocks.append(Rows(part, at(t, xo, yy), first, x_lanes))
        encode(blocks, x_out.at[t])
        x_copy(t).start()

    def n_copy(t, way):
        return remote(
            n_out.at[t, way], n_in.at[t, way], n_send.at[t, way], n_recv.at[t, way], (right, left)[way]
        )

    def p_copy(t, way):
        return remote(
            p_out.at[t, way], p_in.at[t, way], p_send.at[t, way], p_recv.at[t, way], (right, left)[way]
        )

    def w_copy(t):
        return remote(w_out.at[t], w_in.at[t], w_send.at[t], w_recv.at[t], partner)

    def x_copy(t):
        return remote(x_out.at[t], x_in.at[t], x_send.at[t], x_recv.at[t], partner)

    def y_copy(t, way):
        return remote(
            y_out.at[t, way], y_in.at[t, way], y_send.at[t, way], y_recv.at[t, way], (right, left)[way]
        )

    def m_copy(t, way):
        return remote(
            m_out.at[t, way], m_in.at[t, way], m_send.at[t, way], m_recv.at[t, way], (right, left)[way]
        )

    def c_copy(t, block, lane, target):
        spot = scr.at[t, block]
        return remote(spot, spot, c_send.at[t, lane], c_recv.at[t, block], target)

    def at(t, lx, yy):
        return t * (LO * YS) + occ_at(lx, yy)

    def add(block, first, lanes, message, tile, scale):
        for lane in lanes:
            spot = (block, pl.ds(first, HALF), pl.ds(lane, LANE))
            part[spot] = part[spot] + decode(message, tile, scale)
            tile += 1

    def pair_sum(t):
        x_copy(t).wait_recv()
        message = x_in.at[t]
        scale = unit(message, YS * 2 * x_tiles)
        for yy in range(YS):
            for half in range(2):
                add(at(t, lo, yy), half * HALF, x_lanes, message, (yy * 2 + half) * x_tiles, scale)
        for way in range(2):
            beside = (y_next, y_last)[way]
            encode(
                [
                    Rows(part, at(t, lo, y_far), way * HALF, x_lanes),
                    Rows(part, at(t, lo, beside), (1 - way) * HALF, x_lanes),
                ],
                y_out.at[t, way],
            )
            y_copy(t, way).start()

    def pass_on(t):
        for way in range(2):
            beside = (y_next, y_last)[way]
            y_copy(t, way).wait_recv()
            message = y_in.at[t, way]
            add(at(t, lo, beside), way * HALF, x_lanes, message, 0, unit(message, 2 * x_tiles))
            encode([Rows(part, at(t, lo, beside), way * HALF, x_lanes)], m_out.at[t, way])
            m_copy(t, way).start()

    def pass_on_y(t):
        for way in range(2):
            beside = (y_next, y_last)[way]
            n_copy(t, way).wait_recv()
            message = n_in.at[t, way]
            scale = unit(message, 2 * LO * y_tiles)
            for lx in range(LO):
                add(at(t, lx, beside), way * HALF, y_lanes, message, lx * y_tiles, scale)
            encode(
                [Rows(part, at(t, lx, beside), way * HALF, y_lanes) for lx in range(LO)], p_out.at[t, way]
            )
            p_copy(t, way).start()

    def sum_y(t):
        for way in range(2):
            p_copy(t, way).wait_recv()
        for half in range(2):
            near, far = n_in.at[t, 1 - half], p_in.at[t, half]
            near_scale, far_scale = unit(near, 2 * LO * y_tiles), unit(far, LO * y_tiles)
            for lx in range(LO):
                add(at(t, lx, y), half * HALF, y_lanes, near, (LO + lx) * y_tiles, near_scale)
                add(at(t, lx, y), half * HALF, y_lanes, far, lx * y_tiles, far_scale)
        encode([Rows(part, at(t, xo, y), half * HALF, y_lanes) for half in range(2)], w_out.at[t])
        w_copy(t).start()

    def panel(t):
        zz = chunk_z(t)
        for way in range(2):
            m_copy(t, way).wait_recv()
        w_copy(t).wait_recv()
        other = w_in.at[t]
        other_scale = unit(other, 2 * y_tiles)
        for half in range(2):
            near, far = y_in.at[t, 1 - half], m_in.at[t, half]
            near_scale, far_scale = unit(near, 2 * x_tiles), unit(far, x_tiles)
            for lane in range(0, width, LANE):
                total = part[at(t, lo, y), pl.ds(half * HALF, HALF), pl.ds(lane, LANE)]
                tile = lane // LANE
                if tile < x_tiles:
                    total = total + decode(near, x_tiles + tile, near_scale)
                    total = total + decode(far, tile, far_scale)
                else:
                    total = total + decode(other, half * y_tiles + tile - x_tiles, other_scale)
                kept = []
                for h in range(HI):
                    row = pl.multiple_of(h * (Z * CORE * 8) + zz * (CORE * 8) + half * 8, 8)
                    value = prev_ref[pl.ds(row, 8), pl.ds(lane, LANE)] - total[h * 8 : h * 8 + 8]
                    out_ref[pl.ds(row, 8), pl.ds(lane, LANE)] = value
                    kept.append(value)
                scr[t, k, pl.ds(half * HALF, HALF), pl.ds(lane, LANE)] = jnp.concatenate(
                    kept, axis=0
                ).astype(BF16)
        c_copy(t, k, 0, partner).start()
        c_copy(t, k, 1, right).start()
        c_copy(t, k, 2, left).start()

    def await_block(t, block):
        c_copy(t, block, 0, partner).wait_recv()

    def spread_partner(t):
        block = occ_at(xo, y)
        await_block(t, block)
        c_copy(t, block, 3, right).start()
        c_copy(t, block, 4, left).start()

    def spread_right(t):
        block = occ_at(lo, y_last)
        await_block(t, block)
        c_copy(t, block, 5, right).start()

    def spread_left(t):
        block = occ_at(xo, y_next)
        await_block(t, block)
        c_copy(t, block, 6, left).start()

    def energy(t):
        zz = chunk_z(t)
        for block in (occ_at(xo, y_last), occ_at(lo, y_next), occ_at(lo, y_far), occ_at(xo, y_far)):
            await_block(t, block)
        await_sibling(d_set, zz)
        lhs = scr[t].reshape(LO * YS * 2 * HALF, width)
        step = 512
        for first in range(0, s_ref.shape[1], step):
            lanes = pl.ds(first, step)
            applied = jnp.dot(lhs, s_ref[:, lanes], preferred_element_type=F32)
            total = acc[:, lanes]
            for g in range(CORE * HI):
                rows = slab[zz, g // HI, g % HI, :, lanes].astype(F32)
                for kk in range(LO * YS):
                    at = kk * 2 * HALF + g * 8
                    total = total + applied[at : at + 8] * rows[kk * 8 : kk * 8 + 8]
            acc[:, lanes] = total

    start(to_opposite(a_set))
    start(to_line(a_set, z, hi, 0))
    start(to_line(a_set, z, hi, 1))
    start(to_sibling(a_set, z, hi))

    acc[...] = jnp.zeros_like(acc)
    states, orbitals = s3_ref.shape[1:]
    depth = wide.shape[0] // states

    def spread_states(n, carry):
        at_row = pl.multiple_of(n * depth, depth)
        for lane in range(0, orbitals, LANE):
            raw = s3_ref[pl.ds(at_row, depth), :, pl.ds(lane, LANE)].astype(F32)
            wide[...] = raw.reshape(depth * states, LANE)
            for state in range(states):
                s_ref[pl.ds(at_row, depth), pl.ds(state * orbitals + lane, LANE)] = wide[
                    pl.ds(state, depth, stride=states), :
                ].astype(BF16)
        return carry

    lax.fori_loop(0, s3_ref.shape[0] // depth, spread_states, 0)
    slab[z, core, hi] = jnp.dot(chosen, s_ref[...], preferred_element_type=F32).astype(BF16)
    start(to_sibling(d_set, z, hi))

    def to_diagonal():
        return remote(slab.at[z, core, hi], relayed, r_send.at[0], r_recv.at[0], diagonal)

    def relay_on():
        return remote(relayed, slab.at[z, core, 1 - hi], d_opp.at[0], d_recv.at[z, 1 - hi], partner)

    start(to_diagonal())

    def relay(t):
        to_diagonal().wait_recv()
        start(relay_on())

    def first_far(group):
        await_shard(group, z, 1 - hi)
        start(to_line(group, z, 1 - hi, 0))
        start(to_line(group, z, 1 - hi, 1))
        start(to_sibling(group, z, 1 - hi))

    def first_own(t):
        start(to_line(d_set, z, hi, 0))
        start(to_line(d_set, z, hi, 1))

    stages = {
        RELAY: relay,
        A_OPP: lambda t: first_far(a_set),
        D_OWN: first_own,
        D_OPP: lambda t: first_far(d_set),
        A_RING: lambda t: ring(a_set, t, 0, start, True),
        A_RING2: lambda t: ring(a_set, t, 1, start, True),
        D_RING: lambda t: ring(d_set, t, 0, start, True),
        D_RING2: lambda t: ring(d_set, t, 1, start, True),
        PART: panel_part,
        SUM: pair_sum,
        PASS: pass_on,
        PASS_Y: pass_on_y,
        SUM_Y: sum_y,
        PANEL: panel,
        NEAR: spread_partner,
        FAR_R: spread_right,
        FAR_L: spread_left,
        PAIRS: energy,
    }

    def event(n, carry):
        word = jnp.int32(0)
        for at_word in range(0, len(ORDER), 3):
            packed = 0
            for stage, t in reversed(ORDER[at_word : at_word + 3]):
                packed = packed * 256 + stage * CHUNKS + t
            word = jnp.where(n // 3 == at_word // 3, packed, word)
        place = lax.rem(n, 3)
        code = jnp.where(place == 0, word, jnp.where(place == 1, word // 256, word // 65536)) % 256
        for stage, body in stages.items():
            @pl.when(code // CHUNKS == stage)
            def _():
                body(lax.rem(code, CHUNKS))
        return carry

    lax.fori_loop(0, len(ORDER), event, 0)

    pairs = jnp.sum(acc[...], axis=0, keepdims=True)
    mine = hi * CORE + core
    for n in range(state_idx.shape[0]):
        gap = mo_ref[state_idx[n]] - orb_ref[...]
        factor = gap / (gap * gap + 0.25)
        value = jnp.sum(factor * pairs[:, n * orbitals : (n + 1) * orbitals], axis=1, keepdims=True)
        sg_chip[mine, pl.ds(n, 1), :] = jnp.broadcast_to(value, (1, LANE))

    def chip_copy(n, target):
        spot = sg_chip.at[mine]
        return remote(spot, spot, g_send.at[n], g_recv.at[mine], target)

    chip = [
        (sibling, hi * CORE + 1 - core),
        (opposite, (1 - hi) * CORE + core),
        (across, (1 - hi) * CORE + 1 - core),
    ]
    for n, (target, slot) in enumerate(chip):
        chip_copy(n, target).start()
    for n, (target, slot) in enumerate(chip):
        spot = sg_chip.at[slot]
        remote(spot, spot, g_send.at[n], g_recv.at[slot], target).wait_recv()
    sg_line[z] = (sg_chip[0] + sg_chip[1]) + (sg_chip[2] + sg_chip[3])

    def line_copy(n, target):
        spot = sg_line.at[z]
        return remote(spot, spot, l_send.at[n], l_recv.at[z], target)

    for n, target in enumerate(line):
        line_copy(n, target).start()
    for n, target in enumerate(line):
        slot = lax.rem(z + 1 + n, Z)
        spot = sg_line.at[slot]
        remote(spot, spot, l_send.at[n], l_recv.at[slot], target).wait_recv()
    total = sg_line[0]
    for n in range(1, Z):
        total = total + sg_line[n]
    diag = lax.broadcasted_iota(jnp.int32, total.shape, 0) == lax.broadcasted_iota(jnp.int32, total.shape, 1)
    sig_ref[...] = jnp.sum(jnp.where(diag, total, 0.0), axis=0, keepdims=True)[:, : sig_ref.shape[1]]

    for n, (target, slot) in enumerate(chip):
        chip_copy(n, target).wait_send()
    for n, target in enumerate(line):
        line_copy(n, target).wait_send()
    finish(to_opposite(a_set))
    finish(to_diagonal())
    finish(relay_on())
    for group in (a_set, d_set):
        for h in range(HI):
            finish(to_line(group, z, h, 0))
            finish(to_line(group, z, h, 1))
            finish(to_sibling(group, z, h))

        def finish_ring(c, carry):
            ring(group, c, 0, finish, False)
            ring(group, c, 1, finish, False)
            return carry

        lax.fori_loop(1, CHUNKS, finish_ring, 0)

    def drain(t, carry):
        x_copy(t).wait_send()
        for way in range(2):
            y_copy(t, way).wait_send()
            m_copy(t, way).wait_send()
            n_copy(t, way).wait_send()
            p_copy(t, way).wait_send()
        w_copy(t).wait_send()
        for lane in range(7):
            c_copy(t, k, lane, partner).wait_send()
        return carry

    lax.fori_loop(0, CHUNKS, drain, 0)


def local(
    three_index,
    polar_prev,
    states,
    mo_energy,
    vir_energy,
    orbital_energy,
    occ_index,
    state_index,
    slab_rows,
):
    ri_count = lax.axis_size("ri")
    occ_count = lax.axis_size("occ")
    assert (ri_count, occ_count) == (HI * Z * CORE, LO * YS)
    p_dev = three_index.shape[0]
    col_block = polar_prev.shape[0]
    picks = slab_rows.shape[0] // ri_count
    ns_dev, orbitals = states.shape[1:]
    flat = three_index.reshape(p_dev, -1)
    pairs = flat.shape[1]
    spread = ns_dev * orbitals
    y_tiles = Y_FIRST
    x_tiles = p_dev // LANE - Y_FIRST

    def message(count, *lead):
        return pltpu.VMEM((CHUNKS, *lead, count + 1, HALF, LANE), jnp.int16)

    vmem = pl.BlockSpec(memory_space=pltpu.VMEM)
    smem = pl.BlockSpec(memory_space=pltpu.SMEM)
    dma = pltpu.SemaphoreType.DMA
    ring_sems = [dma((Z, HI)), dma((Z, HI)), dma((Z, HI, 3)), dma((1,))]
    panel_out, sig = pl.pallas_call(
        kernel,
        out_shape=(
            jax.ShapeDtypeStruct((col_block, p_dev), F32),
            jax.ShapeDtypeStruct((1, ns_dev), F32),
        ),
        in_specs=[vmem] * 5 + [smem] * 4,
        out_specs=(vmem, vmem),
        scratch_shapes=[
            pltpu.VMEM((Z, CORE, HI, picks, pairs), BF16),
            pltpu.VMEM((Z, CORE, HI, picks, spread), BF16),
            pltpu.VMEM((CHUNKS * occ_count, 2 * HALF, p_dev), F32),
            message(YS * 2 * x_tiles), message(YS * 2 * x_tiles),
            message(2 * x_tiles, 2), message(2 * x_tiles, 2),
            message(x_tiles, 2), message(x_tiles, 2),
            message(2 * LO * y_tiles, 2), message(2 * LO * y_tiles, 2),
            message(LO * y_tiles, 2), message(LO * y_tiles, 2),
            message(2 * y_tiles), message(2 * y_tiles),
            pltpu.VMEM((CHUNKS, occ_count, 2 * HALF, p_dev), BF16),
            pltpu.VMEM((8, spread), F32),
            pltpu.VMEM((HI * CORE, 8, LANE), F32),
            pltpu.VMEM((Z, 8, LANE), F32),
            pltpu.VMEM((p_dev, spread), BF16),
            pltpu.VMEM((LANE * ns_dev, LANE), F32),
            pltpu.VMEM((picks, spread), BF16),
            *ring_sems,
            *ring_sems,
            dma((CHUNKS,)), dma((CHUNKS,)),
            dma((CHUNKS, 2)), dma((CHUNKS, 2)),
            dma((CHUNKS, 2)), dma((CHUNKS, 2)),
            dma((CHUNKS, 2)), dma((CHUNKS, 2)),
            dma((CHUNKS, 2)), dma((CHUNKS, 2)),
            dma((CHUNKS,)), dma((CHUNKS,)),
            dma((CHUNKS, 7)), dma((CHUNKS, occ_count)),
            dma((3,)), dma((HI * CORE,)),
            dma((Z - 1,)), dma((Z,)),
            dma((1,)), dma((1,)),
        ],
        compiler_params=pltpu.CompilerParams(
            collective_id=0, has_side_effects=True, vmem_limit_bytes=60 * 2**20
        ),
        cost_estimate=pl.CostEstimate(
            flops=13 * 10**9, bytes_accessed=9 * 2**20, transcendentals=0
        ),
    )(
        flat, states, polar_prev,
        vir_energy.reshape(1, -1), orbital_energy.reshape(1, -1),
        mo_energy, occ_index, state_index, slab_rows,
    )
    return (panel_out, sig.reshape(ns_dev))


def solution(mesh):
    in_specs = (
        P("ri", "occ", None),
        P("occ", "ri"),
        P("ri", "occ", None),
        P(),
        P(),
        P(),
        P("occ"),
        P("occ"),
        P(),
    )
    out_specs = (P("occ", "ri"), P("occ"))
    return jax.shard_map(local, mesh=mesh, in_specs=in_specs, out_specs=out_specs, check_vma=False)
```

time: 532 us -> 126 us (0.24)
  waiting for transfers between devices: 376 us -> 0 us
  Pallas kernels: 0 us -> 118 us
  blocking collectives: 77.4 us -> 0 us
  matrix products: 26.6 us -> 0 us
  local copies, waits for them, and re-layouts: 31.8 us -> 6.26 us
  between operations: 13.9 us -> 0.65 us
    all_gather x4 -> x0, waiting for transfers between devices: 376 us -> none  [the longest x1 171 us: local(): lax.all_gather(three_index, 'occ', axis=1, tiled=True)]
    pallas_call x0 -> x1, Pallas kernels: none -> 118 us  [local(): pl.pallas_call(kernel, out_shape=(jax.ShapeDtypeStruct((col_block, p_dev)...]
    psum x1 -> x0, blocking collectives: 66.2 us -> none  [local(): pair_sum = lax.psum(local_pairs, 'ri')]
    dot_general x2 -> x0, matrix products: 26.6 us -> none  [the longest x1 13.9 us: local(): jnp.einsum('krsP,rksf->Pf', panel_grid, state_grid, preferred_element_typ...]
    reshape x3 -> x0, local copies, waits for them, and re-layouts: 14.4 us -> none  [the longest x1 13.5 us: local(): state_gathered.reshape(ri_count, occ_count, per_sub, ns_dev * orbitals)]
    all_to_all x1 -> x0, blocking collectives: 11.2 us -> none  [local(): lax.all_to_all(scaled, 'occ', split_axis=0, concat_axis=1, tiled=True)]
    gather x2 -> x0, local copies, waits for them, and re-layouts: 5.78 us -> none  [the longest x1 3.49 us: local(): state_rows = states[local_rows]]
    unnamed x12 -> x5, local copies, waits for them, and re-layouts: 10.9 us -> 6.26 us
  transfers between devices with their start and end apart: 4 -> 0, of which waited for: 4 -> 0; matrix products, arithmetic and copies ran while one was open for 8% -> 0% of each run, Pallas kernels for 0% -> 0%
where the time goes in v1:
time: 126 us; the launch traced here: 125 us
  Pallas kernels  118 us (94%)
  local copies, waits for them, and re-layouts  6.26 us (5%)
    pallas_call x1, Pallas kernels, local(): pl.pallas_call(kernel, out_shape=(jax.ShapeDtypeStruct((col_block, p_dev)...  118 us
    unnamed x5, local copies, waits for them, and re-layouts  6.26 us

profile of v1, /device:TPU:1, one launch (start us, length us, event | category | flops | bytes accessed | tf_op | source)
XLA Modules:
  0.0 125.4 jit_solution(15933083799164997805)
XLA Ops:
  0.6 3.4 %copy.11 = bf16[128,8,4,256]{3,1,2,0:T(8,128)(2,1)} copy(bf16[128,8,4,256]{3,2,1,0:T(4,128)(2,1)} %bitcast.5) | data formatting | bytes 4194304
  4.1 118.5 %shard_map.104 = (f32[256,1024]{1,0:T(8,128)}, f32[1,8]{1,0:T(1,128)}) custom-call(bf16[1024,1024]{1,0:T(8,128)(2,1)} %bitcast.6, bf16[1024,8,256]{2,1,0:T(8,128)(2,1)} %s3_ref.1, f32[256,1024]{1,0:T(8,128)} %prev_ref.1, f32[1,256]{1,0:T(1,128)} %bitcast.7, f32[1,256]{1,0:T(1,128)} %bitcast.8, f32[1024]{0:T(1024)} %mo_ref.1, s32[4]{0:T(128)} %occ_idx.1, ...), custom_call_target="tpu_custom_call" | custom-call | flops 12999999488 | bytes 9437184 | tf_op jit(solution)/shard_map/pallas_call | solution.py:583
  122.6 0.0 copy-start
  122.6 2.3 %copy.14 = f32[256,1024]{1,0:T(8,128)} copy(f32[256,1024]{1,0:T(8,128)} %get-tuple-element.8) | data formatting | bytes 2097152
  124.9 0.0 copy-done
  124.9 0.5 copy.15
Async XLA Ops:
  122.6 2.3 %copy-start = (f32[1,8]{1,0:T(1,128)S(1)}, f32[1,8]{1,0:T(1,128)}, u32[]{:S(2)}) copy-start(f32[1,8]{1,0:T(1,128)} %get-tuple-element.5) | copy-start | bytes 100

commit v2 on v1

--- a/solution.py
+++ b/solution.py
@@ -11,26 +11,30 @@
 HALF = 16
 Y_FIRST = 4
 
-STAGES = 19
 (
-    RELAY, A_OPP, D_OWN, D_OPP, A_RING, A_RING2, D_RING, D_RING2, PART, SUM, PASS, PASS_Y, SUM_Y, PANEL,
-    NEAR, FAR_R, FAR_L, PAIRS,
-) = range(1, STAGES)
+    RELAY, A_OPP, D_PREP, D_OWN, D_OPP, A_RING, A_RING2, D_RING, D_RING2, PART_Y, PART_X, SUM, PASS, PASS_Y,
+    SUM_Y, PANEL, NEAR, FAR_R, FAR_L, PAIRS,
+) = range(20)
 ORDER = (
-    (A_RING, 1), (A_RING, 2), (A_OPP, 0), (PART, 0), (A_RING, 3), (A_RING, 4), (A_RING2, 1), (A_RING2, 2),
-    (RELAY, 0), (PASS_Y, 0), (SUM_Y, 0), (SUM, 0), (PART, 1), (PART, 2), (A_RING2, 3), (D_OWN, 0),
-    (A_RING2, 4), (A_RING, 5), (A_RING, 6), (PASS, 0), (PASS_Y, 1), (PANEL, 0), (PART, 3), (PASS_Y, 2),
-    (PART, 4), (FAR_R, 0), (SUM_Y, 1), (A_RING2, 6), (SUM_Y, 2), (D_OPP, 0), (PASS_Y, 3), (A_RING2, 5),
-    (A_RING, 7), (PASS_Y, 4), (SUM, 1), (NEAR, 0), (PART, 5), (D_RING, 2), (PART, 6), (SUM_Y, 3), (SUM_Y, 4),
-    (SUM, 2), (A_RING2, 7), (D_RING, 1), (PASS, 1), (FAR_L, 0), (PART, 7), (PANEL, 1), (PASS_Y, 5), (PASS, 2),
-    (D_RING2, 1), (SUM, 3), (PASS_Y, 6), (SUM, 4), (D_RING2, 2), (PANEL, 2), (D_RING, 4), (PAIRS, 0),
-    (SUM_Y, 5), (D_RING, 3), (NEAR, 1), (FAR_R, 1), (PASS, 3), (SUM_Y, 6), (SUM, 5), (PASS, 4), (PASS_Y, 7),
-    (FAR_R, 2), (SUM, 6), (PANEL, 3), (D_RING2, 3), (NEAR, 2), (SUM, 7), (PANEL, 4), (NEAR, 3), (D_RING2, 4),
-    (PASS, 5), (FAR_L, 1), (NEAR, 4), (D_RING, 6), (SUM_Y, 7), (D_RING, 5), (PASS, 6), (PANEL, 5), (PASS, 7),
-    (D_RING2, 6), (FAR_L, 2), (D_RING2, 5), (NEAR, 5), (PANEL, 6), (FAR_R, 3), (FAR_L, 3), (PANEL, 7),
-    (FAR_R, 4), (NEAR, 6), (PAIRS, 1), (FAR_L, 4), (D_RING, 7), (D_RING2, 7), (NEAR, 7), (FAR_R, 5),
-    (PAIRS, 2), (FAR_L, 5), (FAR_R, 6), (PAIRS, 3), (FAR_L, 6), (FAR_R, 7), (PAIRS, 4), (FAR_L, 7),
-    (PAIRS, 5), (PAIRS, 6), (PAIRS, 7),
+    (D_PREP, 0), (A_OPP, 0), (A_RING, 1), (A_RING, 2), (PART_Y, 0), (PART_X, 0), (PASS_Y, 0), (RELAY, 0),
+    (A_RING2, 1), (A_RING2, 2), (A_RING, 3), (A_RING, 4), (SUM_Y, 0), (SUM, 0), (PART_Y, 1), (PART_X, 1),
+    (PART_Y, 2), (PASS, 0), (PART_X, 2), (A_RING2, 3), (A_RING2, 4), (A_RING, 5), (A_RING, 6), (PASS_Y, 1),
+    (PANEL, 0), (PASS_Y, 2), (SUM_Y, 1), (PART_Y, 3), (PART_X, 3), (D_OWN, 0), (A_RING2, 6), (D_OPP, 0),
+    (PART_Y, 4), (PART_X, 4), (SUM_Y, 2), (A_RING2, 5), (FAR_R, 0), (PASS_Y, 3), (A_RING, 7), (SUM, 1),
+    (NEAR, 0), (PASS_Y, 4), (PART_Y, 5), (PART_X, 5), (PART_Y, 6), (PART_X, 6), (PASS, 1), (SUM_Y, 3),
+    (SUM, 2), (SUM_Y, 4), (A_RING2, 7), (FAR_L, 0), (SUM, 3), (PANEL, 1), (PART_Y, 7), (PASS, 2), (PART_X, 7),
+    (SUM, 4), (PASS, 3), (D_RING, 1), (D_RING2, 1), (D_RING, 2), (D_RING2, 2), (PASS_Y, 5), (PASS_Y, 6),
+    (PANEL, 2), (FAR_R, 1), (PAIRS, 0, 0), (PAIRS, 0, 1), (PAIRS, 0, 2), (PAIRS, 0, 3), (PANEL, 3), (NEAR, 1),
+    (SUM, 5), (PASS, 4), (PASS_Y, 7), (SUM_Y, 5), (SUM, 6), (SUM_Y, 6), (NEAR, 2), (PANEL, 4), (NEAR, 3),
+    (SUM, 7), (FAR_R, 2), (PASS, 5), (D_RING, 3), (D_RING2, 3), (D_RING, 4), (D_RING2, 4), (NEAR, 4),
+    (SUM_Y, 7), (FAR_L, 1), (PASS, 6), (FAR_R, 3), (FAR_L, 2), (PANEL, 5), (PASS, 7), (FAR_L, 3), (PANEL, 6),
+    (NEAR, 5), (FAR_L, 4), (PAIRS, 1, 0), (FAR_R, 4), (PAIRS, 1, 1), (NEAR, 6), (PAIRS, 1, 2), (PANEL, 7),
+    (PAIRS, 1, 3), (D_RING, 5), (D_RING2, 5), (D_RING, 6), (D_RING2, 6), (PAIRS, 2, 0), (PAIRS, 2, 1),
+    (NEAR, 7), (PAIRS, 2, 2), (PAIRS, 2, 3), (FAR_R, 5), (PAIRS, 3, 0), (PAIRS, 3, 1), (FAR_R, 6),
+    (PAIRS, 3, 2), (FAR_L, 5), (PAIRS, 3, 3), (D_RING, 7), (D_RING2, 7), (FAR_L, 6), (PAIRS, 4, 0),
+    (PAIRS, 4, 1), (PAIRS, 4, 2), (FAR_L, 7), (FAR_R, 7), (PAIRS, 4, 3), (PAIRS, 5, 0), (PAIRS, 5, 1),
+    (PAIRS, 5, 2), (PAIRS, 5, 3), (PAIRS, 6, 0), (PAIRS, 6, 1), (PAIRS, 6, 2), (PAIRS, 6, 3), (PAIRS, 7, 0),
+    (PAIRS, 7, 1), (PAIRS, 7, 2), (PAIRS, 7, 3),
 )
 
 MESH = pl.DeviceIdType.MESH
@@ -46,7 +50,6 @@
 
 
 def tile_scale(peak):
-    peak = jnp.max(jnp.max(peak, axis=0, keepdims=True), axis=1, keepdims=True)
     return jnp.floor(jnp.log(jnp.maximum(peak, 1e-20) * 1.001) * 1.4426950408889634) + 1.0
 
 
@@ -61,9 +64,9 @@
     at = 0
     for load in blocks:
         for lane in load.lanes:
-            message[at] = jnp.round(load(lane) * inverse).astype(jnp.int32).astype(jnp.int16)
+            message[at] = (load(lane) * inverse).astype(jnp.int32).astype(jnp.int16)
             at += 1
-    message[at] = jnp.broadcast_to(exponent, (HALF, LANE)).astype(jnp.int32).astype(jnp.int16)
+    message[at] = exponent.astype(jnp.int32).astype(jnp.int16)
 
 
 def unit(message, last):
@@ -83,13 +86,13 @@
 
 
 def kernel(
-    x_ref, s3_ref, prev_ref, vir_ref, orb_ref, mo_ref, occ_idx, state_idx, slab_rows,
+    x_ref, s3_hbm, prev_hbm, vir_ref, orb_ref, mo_ref, occ_idx, state_idx, slab_rows,
     out_ref, sig_ref,
     cols, slab, part, x_out, x_in, y_out, y_in, m_out, m_in, n_out, n_in, p_out, p_in, w_out, w_in,
-    scr, acc, sg_chip, sg_line, s_ref, wide, relayed,
+    scr, acc, sg_chip, sg_line, s_ref, wide, relayed, s3_ref, prev_ref,
     a_recv, a_sib, a_send, a_opp, d_recv, d_sib, d_send, d_opp,
     x_send, x_recv, y_send, y_recv, m_send, m_recv, n_send, n_recv, p_send, p_recv, w_send, w_recv,
-    c_send, c_recv, g_send, g_recv, l_send, l_recv, r_send, r_recv,
+    c_send, c_recv, g_send, g_recv, l_send, l_recv, r_send, r_recv, load,
 ):
     width = prev_ref.shape[1]
     x_lanes = range(0, width - Y_FIRST * LANE, LANE)
@@ -120,10 +123,15 @@
     right, left = (ri, occ_at(lo, y_next)), (ri, occ_at(lo, y_last))
     line = [(ri_at(hi, lax.rem(z + s, Z), core), k) for s in range(1, Z)]
 
+    s3_copy = pltpu.make_async_copy(s3_hbm, s3_ref, load.at[0])
+    prev_copy = pltpu.make_async_copy(prev_hbm, prev_ref, load.at[1])
     barrier = pltpu.get_barrier_semaphore()
     friends = [sibling, opposite, across, partner, diagonal, right, left] + line
     for friend in friends:
         pl.semaphore_signal(barrier, inc=1, device_id=friend, device_id_type=MESH)
+
+    s3_copy.start()
+    prev_copy.start()
 
     per_sub = prev_ref.shape[0] // (HI * Z * CORE)
     picks = LO * YS * per_sub
@@ -161,8 +169,7 @@
     def to_line(group, zz, h, way):
         buf, recv, sib, send, opp = group
         shard = buf.at[zz, core, h]
-        ahead = (ri_at(hi, lax.rem(z + jnp.where(way == 0, 1, Z - 1), Z), core), k)
-        return remote(shard, shard, send.at[zz, h, way], recv.at[zz, h], ahead)
+        return remote(shard, shard, send.at[zz, h, way], recv.at[zz, h], (up, down)[way])
 
     def to_sibling(group, zz, h):
         buf, recv, sib, send, opp = group
@@ -183,12 +190,10 @@
     def ring(group, c, far, act, arrive):
         zz = chunk_z(c)
         h = 1 - hi if far else hi
-        way = lax.rem(c + 1, 2)
+        way = (c + 1) % 2
         if arrive:
             await_shard(group, zz, h)
-
-        @pl.when(jnp.logical_or(c < 5, jnp.logical_and(c < 7, way == far)))
-        def _():
+        if c < 5 or (c < 7 and way == far):
             act(to_line(group, zz, h, way))
 
         act(to_sibling(group, zz, h))
@@ -200,15 +205,16 @@
         copy.wait_send()
 
     def chunk_z(t):
+        if isinstance(t, int):
+            return lax.rem(z + (Z - (t + 1) // 2 if t % 2 else t // 2), Z)
         return lax.rem(z + jnp.where(lax.rem(t, 2) == 1, Z - (t + 1) // 2, t // 2), Z)
 
-    def panel_part(t):
+    def products(t, lanes):
         zz = chunk_z(t)
-        await_sibling(a_set, zz)
         shards = CORE * HI
         lhs = cols[zz].reshape(shards * picks, cols.shape[-1])
         step = 256
-        for first in range(0, width, step):
+        for first in range(lanes.start, lanes.stop, step):
             res = lax.dot_general(
                 lhs, x_ref[pl.ds(first, step), :], (((1,), (1,)), ((), ())),
                 preferred_element_type=F32,
@@ -218,12 +224,19 @@
                     part[t * (LO * YS) + kk, pl.ds(g * 8, 8), pl.ds(first, step)] = res[
                         g * picks + kk * 8 : g * picks + kk * 8 + 8
                     ]
+
+    def part_y(t):
+        await_sibling(a_set, chunk_z(t))
+        products(t, y_lanes)
         for way in range(2):
             beside = (y_next, y_last)[way]
             blocks = [Rows(part, at(t, lx, y_far), way * HALF, y_lanes) for lx in range(LO)]
             blocks += [Rows(part, at(t, lx, beside), (1 - way) * HALF, y_lanes) for lx in range(LO)]
             encode(blocks, n_out.at[t, way])
             n_copy(t, way).start()
+
+    def part_x(t):
+        products(t, x_lanes)
         blocks = []
         for yy in range(YS):
             for first in (0, HALF):
@@ -327,6 +340,8 @@
         for way in range(2):
             m_copy(t, way).wait_recv()
         w_copy(t).wait_recv()
+        if t == 0:
+            prev_copy.wait()
         other = w_in.at[t]
         other_scale = unit(other, 2 * y_tiles)
         for half in range(2):
@@ -372,23 +387,23 @@
         await_block(t, block)
         c_copy(t, block, 6, left).start()
 
-    def energy(t):
+    def energy(t, quarter):
         zz = chunk_z(t)
-        for block in (occ_at(xo, y_last), occ_at(lo, y_next), occ_at(lo, y_far), occ_at(xo, y_far)):
-            await_block(t, block)
-        await_sibling(d_set, zz)
+        if quarter == 0:
+            for block in (occ_at(xo, y_last), occ_at(lo, y_next), occ_at(lo, y_far), occ_at(xo, y_far)):
+                await_block(t, block)
+            await_sibling(d_set, zz)
         lhs = scr[t].reshape(LO * YS * 2 * HALF, width)
-        step = 512
-        for first in range(0, s_ref.shape[1], step):
-            lanes = pl.ds(first, step)
-            applied = jnp.dot(lhs, s_ref[:, lanes], preferred_element_type=F32)
-            total = acc[:, lanes]
-            for g in range(CORE * HI):
-                rows = slab[zz, g // HI, g % HI, :, lanes].astype(F32)
-                for kk in range(LO * YS):
-                    at = kk * 2 * HALF + g * 8
-                    total = total + applied[at : at + 8] * rows[kk * 8 : kk * 8 + 8]
-            acc[:, lanes] = total
+        step = s_ref.shape[1] // 4
+        lanes = pl.ds(quarter * step, step)
+        applied = jnp.dot(lhs, s_ref[:, lanes], preferred_element_type=F32)
+        total = acc[:, lanes]
+        for g in range(CORE * HI):
+            rows = slab[zz, g // HI, g % HI, :, lanes].astype(F32)
+            for kk in range(LO * YS):
+                spot = kk * 2 * HALF + g * 8
+                total = total + applied[spot : spot + 8] * rows[kk * 8 : kk * 8 + 8]
+        acc[:, lanes] = total
 
     start(to_opposite(a_set))
     start(to_line(a_set, z, hi, 0))
@@ -396,23 +411,6 @@
     start(to_sibling(a_set, z, hi))
 
     acc[...] = jnp.zeros_like(acc)
-    states, orbitals = s3_ref.shape[1:]
-    depth = wide.shape[0] // states
-
-    def spread_states(n, carry):
-        at_row = pl.multiple_of(n * depth, depth)
-        for lane in range(0, orbitals, LANE):
-            raw = s3_ref[pl.ds(at_row, depth), :, pl.ds(lane, LANE)].astype(F32)
-            wide[...] = raw.reshape(depth * states, LANE)
-            for state in range(states):
-                s_ref[pl.ds(at_row, depth), pl.ds(state * orbitals + lane, LANE)] = wide[
-                    pl.ds(state, depth, stride=states), :
-                ].astype(BF16)
-        return carry
-
-    lax.fori_loop(0, s3_ref.shape[0] // depth, spread_states, 0)
-    slab[z, core, hi] = jnp.dot(chosen, s_ref[...], preferred_element_type=F32).astype(BF16)
-    start(to_sibling(d_set, z, hi))
 
     def to_diagonal():
         return remote(slab.at[z, core, hi], relayed, r_send.at[0], r_recv.at[0], diagonal)
@@ -420,7 +418,25 @@
     def relay_on():
         return remote(relayed, slab.at[z, core, 1 - hi], d_opp.at[0], d_recv.at[z, 1 - hi], partner)
 
-    start(to_diagonal())
+    def prepare_states(t):
+        states, orbitals = s3_ref.shape[1:]
+        depth = wide.shape[0] // states
+        s3_copy.wait()
+
+        def spread_states(n, carry):
+            at_row = pl.multiple_of(n * depth, depth)
+            for lane in range(0, orbitals, LANE):
+                raw = s3_ref[pl.ds(at_row, depth), :, pl.ds(lane, LANE)].astype(F32)
+                wide[...] = raw.reshape(depth * states, LANE)
+                for state in range(states):
+                    s_ref[pl.ds(at_row, depth), pl.ds(state * orbitals + lane, LANE)] = wide[
+                        pl.ds(state, depth, stride=states), :
+                    ].astype(BF16)
+            return carry
+
+        lax.fori_loop(0, s3_ref.shape[0] // depth, spread_states, 0)
+        slab[z, core, hi] = jnp.dot(chosen, s_ref[...], preferred_element_type=F32).astype(BF16)
+        start(to_diagonal())
 
     def relay(t):
         to_diagonal().wait_recv()
@@ -428,11 +444,12 @@
 
     def first_far(group):
         await_shard(group, z, 1 - hi)
+        start(to_sibling(group, z, 1 - hi))
         start(to_line(group, z, 1 - hi, 0))
         start(to_line(group, z, 1 - hi, 1))
-        start(to_sibling(group, z, 1 - hi))
 
     def first_own(t):
+        start(to_sibling(d_set, z, hi))
         start(to_line(d_set, z, hi, 0))
         start(to_line(d_set, z, hi, 1))
 
@@ -445,7 +462,9 @@
         A_RING2: lambda t: ring(a_set, t, 1, start, True),
         D_RING: lambda t: ring(d_set, t, 0, start, True),
         D_RING2: lambda t: ring(d_set, t, 1, start, True),
-        PART: panel_part,
+        D_PREP: prepare_states,
+        PART_Y: part_y,
+        PART_X: part_x,
         SUM: pair_sum,
         PASS: pass_on,
         PASS_Y: pass_on_y,
@@ -457,25 +476,12 @@
         PAIRS: energy,
     }
 
-    def event(n, carry):
-        word = jnp.int32(0)
-        for at_word in range(0, len(ORDER), 3):
-            packed = 0
-            for stage, t in reversed(ORDER[at_word : at_word + 3]):
-                packed = packed * 256 + stage * CHUNKS + t
-            word = jnp.where(n // 3 == at_word // 3, packed, word)
-        place = lax.rem(n, 3)
-        code = jnp.where(place == 0, word, jnp.where(place == 1, word // 256, word // 65536)) % 256
-        for stage, body in stages.items():
-            @pl.when(code // CHUNKS == stage)
-            def _():
-                body(lax.rem(code, CHUNKS))
-        return carry
-
-    lax.fori_loop(0, len(ORDER), event, 0)
+    for stage, *spot in ORDER:
+        stages[stage](*spot)
 
     pairs = jnp.sum(acc[...], axis=0, keepdims=True)
     mine = hi * CORE + core
+    orbitals = orb_ref.shape[1]
     for n in range(state_idx.shape[0]):
         gap = mo_ref[state_idx[n]] - orb_ref[...]
         factor = gap / (gap * gap + 0.25)
@@ -527,12 +533,9 @@
             finish(to_line(group, z, h, 1))
             finish(to_sibling(group, z, h))
 
-        def finish_ring(c, carry):
+        for c in range(1, CHUNKS):
             ring(group, c, 0, finish, False)
             ring(group, c, 1, finish, False)
-            return carry
-
-        lax.fori_loop(1, CHUNKS, finish_ring, 0)
 
     def drain(t, carry):
         x_copy(t).wait_send()
@@ -577,6 +580,7 @@
         return pltpu.VMEM((CHUNKS, *lead, count + 1, HALF, LANE), jnp.int16)
 
     vmem = pl.BlockSpec(memory_space=pltpu.VMEM)
+    hbm = pl.BlockSpec(memory_space=pl.ANY)
     smem = pl.BlockSpec(memory_space=pltpu.SMEM)
     dma = pltpu.SemaphoreType.DMA
     ring_sems = [dma((Z, HI)), dma((Z, HI)), dma((Z, HI, 3)), dma((1,))]
@@ -586,7 +590,7 @@
             jax.ShapeDtypeStruct((col_block, p_dev), F32),
             jax.ShapeDtypeStruct((1, ns_dev), F32),
         ),
-        in_specs=[vmem] * 5 + [smem] * 4,
+        in_specs=[vmem, hbm, hbm, vmem, vmem] + [smem] * 4,
         out_specs=(vmem, vmem),
         scratch_shapes=[
             pltpu.VMEM((Z, CORE, HI, picks, pairs), BF16),
@@ -605,6 +609,8 @@
             pltpu.VMEM((p_dev, spread), BF16),
             pltpu.VMEM((LANE * ns_dev, LANE), F32),
             pltpu.VMEM((picks, spread), BF16),
+            pltpu.VMEM((p_dev, ns_dev, orbitals), BF16),
+            pltpu.VMEM((col_block, p_dev), F32),
             *ring_sems,
             *ring_sems,
             dma((CHUNKS,)), dma((CHUNKS,)),
@@ -616,7 +622,7 @@
             dma((CHUNKS, 7)), dma((CHUNKS, occ_count)),
             dma((3,)), dma((HI * CORE,)),
             dma((Z - 1,)), dma((Z,)),
-            dma((1,)), dma((1,)),
+            dma((1,)), dma((1,)), dma((2,)),
         ],
         compiler_params=pltpu.CompilerParams(
             collective_id=0, has_side_effects=True, vmem_limit_bytes=60 * 2**20

time: 126 us -> 114 us (0.905)
  Pallas kernels: 118 us -> 107 us
    pallas_call x1, Pallas kernels: 118 us -> 107 us  [local(): pl.pallas_call(kernel, out_shape=(jax.ShapeDtypeStruct((col_block, p_dev)...]
where the time goes in v2:
time: 114 us
  Pallas kernels  107 us (94%)
  local copies, waits for them, and re-layouts  6.26 us (5%)
    pallas_call x1, Pallas kernels, local(): pl.pallas_call(kernel, out_shape=(jax.ShapeDtypeStruct((col_block, p_dev)...  107 us
    unnamed x5, local copies, waits for them, and re-layouts  6.26 us

profile of v2, /device:TPU:1, one launch (start us, length us, event | category | flops | bytes accessed | tf_op | source)
XLA Modules:
  0.0 113.6 jit_solution(3676221514765677178)
XLA Ops:
  0.6 3.4 %copy.11 = bf16[128,8,4,256]{3,1,2,0:T(8,128)(2,1)} copy(bf16[128,8,4,256]{3,2,1,0:T(4,128)(2,1)} %bitcast.5) | data formatting | bytes 4194304
  4.1 106.7 %shard_map.104 = (f32[256,1024]{1,0:T(8,128)}, f32[1,8]{1,0:T(1,128)}) custom-call(bf16[1024,1024]{1,0:T(8,128)(2,1)} %bitcast.6, bf16[1024,8,256]{2,1,0:T(8,128)(2,1)} %s3_hbm.1, f32[256,1024]{1,0:T(8,128)} %prev_hbm.1, f32[1,256]{1,0:T(1,128)} %bitcast.7, f32[1,256]{1,0:T(1,128)} %bitcast.8, f32[1024]{0:T(1024)} %mo_ref.1, s32[4]{0:T(128)} %occ_idx.1, ...), custom_call_target="tpu_custom_call" | custom-call | flops 12999999488 | bytes 9437184 | tf_op jit(solution)/shard_map/pallas_call | solution.py:587
  110.8 0.0 copy-start
  110.8 2.3 %copy.14 = f32[256,1024]{1,0:T(8,128)} copy(f32[256,1024]{1,0:T(8,128)} %get-tuple-element.8) | data formatting | bytes 2097152
  113.1 0.0 copy-done
  113.1 0.5 copy.15
Async XLA Ops:
  110.8 2.3 %copy-start = (f32[1,8]{1,0:T(1,128)S(1)}, f32[1,8]{1,0:T(1,128)}, u32[]{:S(2)}) copy-start(f32[1,8]{1,0:T(1,128)} %get-tuple-element.5) | copy-start | bytes 100

commit v3 on v2

--- a/solution.py
+++ b/solution.py
@@ -16,25 +16,25 @@
     SUM_Y, PANEL, NEAR, FAR_R, FAR_L, PAIRS,
 ) = range(20)
 ORDER = (
-    (D_PREP, 0), (A_OPP, 0), (A_RING, 1), (A_RING, 2), (PART_Y, 0), (PART_X, 0), (PASS_Y, 0), (RELAY, 0),
-    (A_RING2, 1), (A_RING2, 2), (A_RING, 3), (A_RING, 4), (SUM_Y, 0), (SUM, 0), (PART_Y, 1), (PART_X, 1),
-    (PART_Y, 2), (PASS, 0), (PART_X, 2), (A_RING2, 3), (A_RING2, 4), (A_RING, 5), (A_RING, 6), (PASS_Y, 1),
-    (PANEL, 0), (PASS_Y, 2), (SUM_Y, 1), (PART_Y, 3), (PART_X, 3), (D_OWN, 0), (A_RING2, 6), (D_OPP, 0),
-    (PART_Y, 4), (PART_X, 4), (SUM_Y, 2), (A_RING2, 5), (FAR_R, 0), (PASS_Y, 3), (A_RING, 7), (SUM, 1),
-    (NEAR, 0), (PASS_Y, 4), (PART_Y, 5), (PART_X, 5), (PART_Y, 6), (PART_X, 6), (PASS, 1), (SUM_Y, 3),
-    (SUM, 2), (SUM_Y, 4), (A_RING2, 7), (FAR_L, 0), (SUM, 3), (PANEL, 1), (PART_Y, 7), (PASS, 2), (PART_X, 7),
-    (SUM, 4), (PASS, 3), (D_RING, 1), (D_RING2, 1), (D_RING, 2), (D_RING2, 2), (PASS_Y, 5), (PASS_Y, 6),
-    (PANEL, 2), (FAR_R, 1), (PAIRS, 0, 0), (PAIRS, 0, 1), (PAIRS, 0, 2), (PAIRS, 0, 3), (PANEL, 3), (NEAR, 1),
-    (SUM, 5), (PASS, 4), (PASS_Y, 7), (SUM_Y, 5), (SUM, 6), (SUM_Y, 6), (NEAR, 2), (PANEL, 4), (NEAR, 3),
-    (SUM, 7), (FAR_R, 2), (PASS, 5), (D_RING, 3), (D_RING2, 3), (D_RING, 4), (D_RING2, 4), (NEAR, 4),
-    (SUM_Y, 7), (FAR_L, 1), (PASS, 6), (FAR_R, 3), (FAR_L, 2), (PANEL, 5), (PASS, 7), (FAR_L, 3), (PANEL, 6),
-    (NEAR, 5), (FAR_L, 4), (PAIRS, 1, 0), (FAR_R, 4), (PAIRS, 1, 1), (NEAR, 6), (PAIRS, 1, 2), (PANEL, 7),
-    (PAIRS, 1, 3), (D_RING, 5), (D_RING2, 5), (D_RING, 6), (D_RING2, 6), (PAIRS, 2, 0), (PAIRS, 2, 1),
-    (NEAR, 7), (PAIRS, 2, 2), (PAIRS, 2, 3), (FAR_R, 5), (PAIRS, 3, 0), (PAIRS, 3, 1), (FAR_R, 6),
-    (PAIRS, 3, 2), (FAR_L, 5), (PAIRS, 3, 3), (D_RING, 7), (D_RING2, 7), (FAR_L, 6), (PAIRS, 4, 0),
-    (PAIRS, 4, 1), (PAIRS, 4, 2), (FAR_L, 7), (FAR_R, 7), (PAIRS, 4, 3), (PAIRS, 5, 0), (PAIRS, 5, 1),
-    (PAIRS, 5, 2), (PAIRS, 5, 3), (PAIRS, 6, 0), (PAIRS, 6, 1), (PAIRS, 6, 2), (PAIRS, 6, 3), (PAIRS, 7, 0),
-    (PAIRS, 7, 1), (PAIRS, 7, 2), (PAIRS, 7, 3),
+    (D_PREP, 0), (A_RING, 1), (A_RING, 2), (A_OPP, 0), (PART_Y, 0), (PART_X, 0), (PASS_Y, 0), (A_RING, 3),
+    (A_RING, 4), (A_RING2, 1), (A_RING2, 2), (RELAY, 0), (SUM, 0), (SUM_Y, 0), (PART_Y, 1), (PART_X, 1),
+    (PASS, 0), (PART_Y, 2), (PART_X, 2), (A_RING, 5), (A_RING, 6), (A_RING2, 3), (A_RING2, 4), (PANEL, 0),
+    (PASS_Y, 1), (PASS_Y, 2), (PART_Y, 3), (PART_X, 3), (D_OWN, 0), (A_RING2, 6), (SUM_Y, 1), (FAR_R, 0),
+    (PART_Y, 4), (PART_X, 4), (SUM_Y, 2), (D_OPP, 0), (PASS_Y, 3), (A_RING, 7), (A_RING2, 5), (NEAR, 0),
+    (SUM, 1), (PART_Y, 5), (PART_X, 5), (FAR_L, 0), (PASS_Y, 4), (SUM_Y, 3), (PART_Y, 6), (SUM, 2),
+    (PART_X, 6), (PASS, 1), (A_RING2, 7), (PART_Y, 7), (PASS_Y, 5), (PART_X, 7), (PANEL, 1), (D_RING, 1),
+    (PASS, 2), (SUM_Y, 4), (SUM, 3), (D_RING2, 1), (PAIRS, 0, 0), (D_RING, 2), (PASS_Y, 6), (PAIRS, 0, 1),
+    (SUM, 4), (D_RING2, 2), (PAIRS, 0, 2), (PAIRS, 0, 3), (SUM_Y, 5), (PANEL, 2), (PASS_Y, 7), (PASS, 3),
+    (FAR_R, 1), (SUM_Y, 6), (PASS, 4), (SUM, 5), (FAR_R, 2), (NEAR, 1), (PANEL, 3), (SUM_Y, 7), (PANEL, 4),
+    (SUM, 6), (D_RING, 3), (D_RING2, 3), (NEAR, 2), (D_RING, 4), (D_RING2, 4), (FAR_L, 1), (PASS, 5),
+    (SUM, 7), (NEAR, 3), (NEAR, 4), (PASS, 6), (PANEL, 5), (FAR_R, 3), (FAR_L, 2), (FAR_R, 4), (NEAR, 5),
+    (PASS, 7), (PAIRS, 1, 0), (PANEL, 6), (D_RING, 5), (PAIRS, 1, 1), (PAIRS, 1, 2), (FAR_L, 3), (D_RING2, 5),
+    (D_RING, 6), (FAR_L, 4), (PAIRS, 1, 3), (D_RING2, 6), (NEAR, 6), (PANEL, 7), (PAIRS, 2, 0), (PAIRS, 2, 1),
+    (PAIRS, 2, 2), (NEAR, 7), (D_RING, 7), (FAR_R, 5), (PAIRS, 2, 3), (FAR_L, 5), (D_RING2, 7), (FAR_R, 6),
+    (PAIRS, 3, 0), (PAIRS, 3, 1), (PAIRS, 3, 2), (PAIRS, 3, 3), (FAR_L, 6), (PAIRS, 4, 0), (FAR_R, 7),
+    (PAIRS, 4, 1), (PAIRS, 4, 2), (PAIRS, 4, 3), (FAR_L, 7), (PAIRS, 5, 0), (PAIRS, 5, 1), (PAIRS, 5, 2),
+    (PAIRS, 5, 3), (PAIRS, 6, 0), (PAIRS, 6, 1), (PAIRS, 6, 2), (PAIRS, 6, 3), (PAIRS, 7, 0), (PAIRS, 7, 1),
+    (PAIRS, 7, 2), (PAIRS, 7, 3),
 )
 
 MESH = pl.DeviceIdType.MESH
@@ -86,10 +86,10 @@
 
 
 def kernel(
-    x_ref, s3_hbm, prev_hbm, vir_ref, orb_ref, mo_ref, occ_idx, state_idx, slab_rows,
+    x3_ref, s3_hbm, prev_hbm, vir_ref, orb_ref, mo_ref, occ_idx, state_idx, slab_rows,
     out_ref, sig_ref,
     cols, slab, part, x_out, x_in, y_out, y_in, m_out, m_in, n_out, n_in, p_out, p_in, w_out, w_in,
-    scr, acc, sg_chip, sg_line, s_ref, wide, relayed, s3_ref, prev_ref,
+    scr, acc, sg_chip, sg_line, s_ref, wide, relayed, s3_ref, prev_ref, x_ref, few,
     a_recv, a_sib, a_send, a_opp, d_recv, d_sib, d_send, d_opp,
     x_send, x_recv, y_send, y_recv, m_send, m_recv, n_send, n_recv, p_send, p_recv, w_send, w_recv,
     c_send, c_recv, g_send, g_recv, l_send, l_recv, r_send, r_recv, load,
@@ -135,26 +135,25 @@
 
     per_sub = prev_ref.shape[0] // (HI * Z * CORE)
     picks = LO * YS * per_sub
-    groups = []
-    for kk in range(LO * YS):
-        spot = lax.broadcasted_iota(jnp.int32, (per_sub, LANE), 0)
-        rows = jnp.zeros((per_sub, LANE), jnp.int32)
-        for s in range(per_sub):
-            row = slab_rows[kk * prev_ref.shape[0] + ri * per_sub + s] - ri * x_ref.shape[0]
-            rows = jnp.where(spot == s, row, rows)
-        groups.append(rows)
-    rows = jnp.concatenate(groups, axis=0)
-    place = lax.broadcasted_iota(jnp.int32, (picks, LANE), 1)
-    chosen = jnp.concatenate(
-        [jnp.where(place + lane == rows, 1.0, 0.0) for lane in range(0, x_ref.shape[0], LANE)], axis=1
-    ).astype(BF16)
-    weights = []
-    for i in range(occ_idx.shape[0]):
+    pairs_in, virtual = x3_ref.shape[1:]
+    local_rows = [
+        lax.rem(slab_rows[kk * prev_ref.shape[0] + ri * per_sub + s], x3_ref.shape[0])
+        for kk in range(LO * YS)
+        for s in range(per_sub)
+    ]
+    few_rows = few.reshape(virtual // LANE, picks * 8, LANE)
+    for j, row in enumerate(local_rows):
+        raw = x3_ref[row].astype(F32)
+        for lane in range(0, virtual, LANE):
+            few[lane // LANE, j, pl.ds(0, pairs_in), :] = raw[:, lane : lane + LANE]
+    for i in range(pairs_in):
         gap = vir_ref[...] - mo_ref[occ_idx[i]]
-        weights.append(4.0 * gap / (gap * gap + 0.25))
-    weight = jnp.concatenate(weights, axis=1)
-    picked = jnp.dot(chosen, x_ref[...], preferred_element_type=F32)
-    cols[z, core, hi] = (picked * weight).astype(BF16)
+        weight = 4.0 * gap / (gap * gap + 0.25)
+        for lane in range(0, virtual, LANE):
+            picked = few_rows[lane // LANE, pl.ds(i, picks, stride=8), :]
+            cols[z, core, hi, :, pl.ds(i * virtual + lane, LANE)] = (
+                picked * weight[:, lane : lane + LANE]
+            ).astype(BF16)
 
     pl.semaphore_wait(barrier, len(friends))
 
@@ -410,6 +409,32 @@
     start(to_line(a_set, z, hi, 1))
     start(to_sibling(a_set, z, hi))
 
+    depth = wide.shape[0] // 8
+    wide_rows = wide.reshape(depth, 8, LANE)
+
+    def spread_block(n, carry):
+        at_row = pl.multiple_of(n * depth, depth)
+        for lane in range(0, virtual, LANE):
+            wide_rows[:, pl.ds(0, pairs_in), :] = x3_ref[pl.ds(at_row, depth), :, pl.ds(lane, LANE)].astype(F32)
+            for i in range(pairs_in):
+                x_ref[pl.ds(at_row, depth), pl.ds(i * virtual + lane, LANE)] = wide[
+                    pl.ds(i, depth, stride=8), :
+                ].astype(BF16)
+        return carry
+
+    lax.fori_loop(0, x3_ref.shape[0] // depth, spread_block, 0)
+    groups = []
+    for kk in range(LO * YS):
+        spot = lax.broadcasted_iota(jnp.int32, (per_sub, LANE), 0)
+        rows = jnp.zeros((per_sub, LANE), jnp.int32)
+        for s in range(per_sub):
+            rows = jnp.where(spot == s, local_rows[kk * per_sub + s], rows)
+        groups.append(rows)
+    rows = jnp.concatenate(groups, axis=0)
+    place = lax.broadcasted_iota(jnp.int32, (picks, LANE), 1)
+    chosen = jnp.concatenate(
+        [jnp.where(place + lane == rows, 1.0, 0.0) for lane in range(0, x_ref.shape[0], LANE)], axis=1
+    ).astype(BF16)
     acc[...] = jnp.zeros_like(acc)
 
     def to_diagonal():
@@ -420,7 +445,7 @@
 
     def prepare_states(t):
         states, orbitals = s3_ref.shape[1:]
-        depth = wide.shape[0] // states
+        assert states == 8
         s3_copy.wait()
 
         def spread_states(n, carry):
@@ -570,8 +595,7 @@
     col_block = polar_prev.shape[0]
     picks = slab_rows.shape[0] // ri_count
     ns_dev, orbitals = states.shape[1:]
-    flat = three_index.reshape(p_dev, -1)
-    pairs = flat.shape[1]
+    pairs = three_index.shape[1] * three_index.shape[2]
     spread = ns_dev * orbitals
     y_tiles = Y_FIRST
     x_tiles = p_dev // LANE - Y_FIRST
@@ -611,6 +635,8 @@
             pltpu.VMEM((picks, spread), BF16),
             pltpu.VMEM((p_dev, ns_dev, orbitals), BF16),
             pltpu.VMEM((col_block, p_dev), F32),
+            pltpu.VMEM((p_dev, pairs), BF16),
+            pltpu.VMEM((three_index.shape[2] // LANE, picks, 8, LANE), F32),
             *ring_sems,
             *ring_sems,
             dma((CHUNKS,)), dma((CHUNKS,)),
@@ -631,7 +657,7 @@
             flops=13 * 10**9, bytes_accessed=9 * 2**20, transcendentals=0
         ),
     )(
-        flat, states, polar_prev,
+        three_index, states, polar_prev,
         vir_energy.reshape(1, -1), orbital_energy.reshape(1, -1),
         mo_energy, occ_index, state_index, slab_rows,
     )

time: 114 us -> 113 us (level)
  local copies, waits for them, and re-layouts: 6.26 us -> 3.42 us
    unnamed x5 -> x2, local copies, waits for them, and re-layouts: 6.26 us -> 3.42 us
    pallas_call x1, Pallas kernels: 107 us -> 108 us  [local(): pl.pallas_call(kernel, out_shape=(jax.ShapeDtypeStruct((col_block, p_dev)...]
where the time goes in v3:
time: 113 us; the launch traced here: 112 us
  Pallas kernels  108 us (96%)
  local copies, waits for them, and re-layouts  3.42 us (3%)
    pallas_call x1, Pallas kernels, local(): pl.pallas_call(kernel, out_shape=(jax.ShapeDtypeStruct((col_block, p_dev)...  108 us
    unnamed x2, local copies, waits for them, and re-layouts  3.42 us

profile of v3, /device:TPU:1, one launch (start us, length us, event | category | flops | bytes accessed | tf_op | source)
XLA Modules:
  0.0 112.4 jit_solution(10947357424662601232)
XLA Ops:
  0.6 108.3 %shard_map.104 = (f32[256,1024]{1,0:T(8,128)}, f32[1,8]{1,0:T(1,128)}) custom-call(bf16[1024,4,256]{2,1,0:T(4,128)(2,1)} %x3_ref.1, bf16[1024,8,256]{2,1,0:T(8,128)(2,1)} %s3_hbm.1, f32[256,1024]{1,0:T(8,128)} %prev_hbm.1, f32[1,256]{1,0:T(1,128)} %bitcast.3, f32[1,256]{1,0:T(1,128)} %bitcast.4, f32[1024]{0:T(1024)} %mo_ref.1, s32[4]{0:T(128)} %occ_idx.1, ...), custom_call_target="tpu_custom_call" | custom-call | flops 12999999488 | bytes 9437184 | tf_op jit(solution)/shard_map/pallas_call | solution.py:611
  108.9 2.3 %copy.13 = f32[256,1024]{1,0:T(8,128)} copy(f32[256,1024]{1,0:T(8,128)} %get-tuple-element.8) | data formatting | bytes 2097152
  111.3 1.1 copy.14

commit v4 on v3

--- a/solution.py
+++ b/solution.py
@@ -13,28 +13,30 @@
 
 (
     RELAY, A_OPP, D_PREP, D_OWN, D_OPP, A_RING, A_RING2, D_RING, D_RING2, PART_Y, PART_X, SUM, PASS, PASS_Y,
-    SUM_Y, PANEL, NEAR, FAR_R, FAR_L, PAIRS,
-) = range(20)
+    SUM_Y, PANEL, NEAR, FAR_R, FAR_L, PAIRS, X_SPREAD, S_SPREAD,
+) = range(22)
 ORDER = (
-    (D_PREP, 0), (A_RING, 1), (A_RING, 2), (A_OPP, 0), (PART_Y, 0), (PART_X, 0), (PASS_Y, 0), (A_RING, 3),
-    (A_RING, 4), (A_RING2, 1), (A_RING2, 2), (RELAY, 0), (SUM, 0), (SUM_Y, 0), (PART_Y, 1), (PART_X, 1),
-    (PASS, 0), (PART_Y, 2), (PART_X, 2), (A_RING, 5), (A_RING, 6), (A_RING2, 3), (A_RING2, 4), (PANEL, 0),
-    (PASS_Y, 1), (PASS_Y, 2), (PART_Y, 3), (PART_X, 3), (D_OWN, 0), (A_RING2, 6), (SUM_Y, 1), (FAR_R, 0),
-    (PART_Y, 4), (PART_X, 4), (SUM_Y, 2), (D_OPP, 0), (PASS_Y, 3), (A_RING, 7), (A_RING2, 5), (NEAR, 0),
-    (SUM, 1), (PART_Y, 5), (PART_X, 5), (FAR_L, 0), (PASS_Y, 4), (SUM_Y, 3), (PART_Y, 6), (SUM, 2),
-    (PART_X, 6), (PASS, 1), (A_RING2, 7), (PART_Y, 7), (PASS_Y, 5), (PART_X, 7), (PANEL, 1), (D_RING, 1),
-    (PASS, 2), (SUM_Y, 4), (SUM, 3), (D_RING2, 1), (PAIRS, 0, 0), (D_RING, 2), (PASS_Y, 6), (PAIRS, 0, 1),
-    (SUM, 4), (D_RING2, 2), (PAIRS, 0, 2), (PAIRS, 0, 3), (SUM_Y, 5), (PANEL, 2), (PASS_Y, 7), (PASS, 3),
-    (FAR_R, 1), (SUM_Y, 6), (PASS, 4), (SUM, 5), (FAR_R, 2), (NEAR, 1), (PANEL, 3), (SUM_Y, 7), (PANEL, 4),
-    (SUM, 6), (D_RING, 3), (D_RING2, 3), (NEAR, 2), (D_RING, 4), (D_RING2, 4), (FAR_L, 1), (PASS, 5),
-    (SUM, 7), (NEAR, 3), (NEAR, 4), (PASS, 6), (PANEL, 5), (FAR_R, 3), (FAR_L, 2), (FAR_R, 4), (NEAR, 5),
-    (PASS, 7), (PAIRS, 1, 0), (PANEL, 6), (D_RING, 5), (PAIRS, 1, 1), (PAIRS, 1, 2), (FAR_L, 3), (D_RING2, 5),
-    (D_RING, 6), (FAR_L, 4), (PAIRS, 1, 3), (D_RING2, 6), (NEAR, 6), (PANEL, 7), (PAIRS, 2, 0), (PAIRS, 2, 1),
-    (PAIRS, 2, 2), (NEAR, 7), (D_RING, 7), (FAR_R, 5), (PAIRS, 2, 3), (FAR_L, 5), (D_RING2, 7), (FAR_R, 6),
-    (PAIRS, 3, 0), (PAIRS, 3, 1), (PAIRS, 3, 2), (PAIRS, 3, 3), (FAR_L, 6), (PAIRS, 4, 0), (FAR_R, 7),
-    (PAIRS, 4, 1), (PAIRS, 4, 2), (PAIRS, 4, 3), (FAR_L, 7), (PAIRS, 5, 0), (PAIRS, 5, 1), (PAIRS, 5, 2),
-    (PAIRS, 5, 3), (PAIRS, 6, 0), (PAIRS, 6, 1), (PAIRS, 6, 2), (PAIRS, 6, 3), (PAIRS, 7, 0), (PAIRS, 7, 1),
-    (PAIRS, 7, 2), (PAIRS, 7, 3),
+    (X_SPREAD, 4), (X_SPREAD, 5), (X_SPREAD, 6), (X_SPREAD, 7), (X_SPREAD, 0), (X_SPREAD, 1), (X_SPREAD, 2),
+    (X_SPREAD, 3), (D_PREP, 0), (A_RING, 1), (A_RING, 2), (A_OPP, 0), (S_SPREAD, 0), (S_SPREAD, 1),
+    (S_SPREAD, 2), (PART_Y, 0), (PART_X, 0), (S_SPREAD, 3), (S_SPREAD, 4), (PASS_Y, 0), (RELAY, 0),
+    (A_RING2, 1), (A_RING2, 2), (A_RING, 3), (A_RING, 4), (S_SPREAD, 5), (S_SPREAD, 6), (SUM, 0), (SUM_Y, 0),
+    (PART_Y, 1), (PART_Y, 2), (PART_X, 1), (PASS, 0), (PART_X, 2), (S_SPREAD, 7), (A_RING2, 3), (A_RING2, 4),
+    (A_RING, 5), (A_RING, 6), (D_OWN, 0), (PASS_Y, 1), (PANEL, 0), (PASS_Y, 2), (PART_Y, 3), (PART_Y, 4),
+    (D_OPP, 0), (PART_X, 3), (FAR_R, 0), (PART_X, 4), (SUM_Y, 1), (SUM_Y, 2), (NEAR, 0), (A_RING2, 6),
+    (PASS_Y, 3), (SUM, 1), (PASS_Y, 4), (FAR_L, 0), (A_RING2, 5), (SUM, 2), (A_RING, 7), (PART_Y, 5),
+    (PART_Y, 6), (PASS, 1), (PART_X, 5), (PASS, 2), (PART_X, 6), (D_RING, 2), (SUM, 3), (SUM, 4), (D_RING, 1),
+    (A_RING2, 7), (SUM_Y, 3), (PANEL, 1), (SUM_Y, 4), (PAIRS, 0, 0), (PASS_Y, 5), (D_RING2, 1), (PANEL, 2),
+    (PAIRS, 0, 1), (PART_Y, 7), (D_RING2, 2), (PART_X, 7), (PASS, 3), (PASS_Y, 6), (PAIRS, 0, 2), (PASS, 4),
+    (PAIRS, 0, 3), (SUM_Y, 5), (PANEL, 3), (FAR_R, 1), (SUM, 5), (PANEL, 4), (FAR_R, 2), (SUM_Y, 6),
+    (D_RING, 4), (NEAR, 1), (PASS_Y, 7), (NEAR, 2), (D_RING, 3), (D_RING2, 3), (SUM, 6), (D_RING2, 4),
+    (PASS, 5), (NEAR, 3), (NEAR, 4), (SUM, 7), (FAR_L, 1), (SUM_Y, 7), (FAR_R, 3), (FAR_L, 2), (D_RING, 6),
+    (PANEL, 5), (FAR_R, 4), (D_RING, 5), (PASS, 6), (FAR_L, 3), (D_RING2, 6), (D_RING2, 5), (NEAR, 5),
+    (FAR_L, 4), (PASS, 7), (PAIRS, 1, 0), (PAIRS, 1, 1), (PAIRS, 1, 2), (PAIRS, 1, 3), (PANEL, 6),
+    (PAIRS, 2, 0), (PAIRS, 2, 1), (PAIRS, 2, 2), (PAIRS, 2, 3), (PANEL, 7), (D_RING, 7), (NEAR, 6),
+    (D_RING2, 7), (FAR_R, 5), (PAIRS, 3, 0), (FAR_L, 5), (NEAR, 7), (PAIRS, 3, 1), (PAIRS, 3, 2),
+    (PAIRS, 3, 3), (PAIRS, 4, 0), (PAIRS, 4, 1), (PAIRS, 4, 2), (FAR_R, 6), (PAIRS, 4, 3), (FAR_L, 6),
+    (FAR_R, 7), (PAIRS, 5, 0), (FAR_L, 7), (PAIRS, 5, 1), (PAIRS, 5, 2), (PAIRS, 5, 3), (PAIRS, 6, 0),
+    (PAIRS, 6, 1), (PAIRS, 6, 2), (PAIRS, 6, 3), (PAIRS, 7, 0), (PAIRS, 7, 1), (PAIRS, 7, 2), (PAIRS, 7, 3),
 )
 
 MESH = pl.DeviceIdType.MESH
@@ -87,12 +89,12 @@
 
 def kernel(
     x3_ref, s3_hbm, prev_hbm, vir_ref, orb_ref, mo_ref, occ_idx, state_idx, slab_rows,
-    out_ref, sig_ref,
+    out_hbm, sig_ref,
     cols, slab, part, x_out, x_in, y_out, y_in, m_out, m_in, n_out, n_in, p_out, p_in, w_out, w_in,
-    scr, acc, sg_chip, sg_line, s_ref, wide, relayed, s3_ref, prev_ref, x_ref, few,
+    scr, acc, sg_chip, sg_line, s_ref, wide, relayed, s3_ref, prev_ref, x_ref, few, out_ref,
     a_recv, a_sib, a_send, a_opp, d_recv, d_sib, d_send, d_opp,
     x_send, x_recv, y_send, y_recv, m_send, m_recv, n_send, n_recv, p_send, p_recv, w_send, w_recv,
-    c_send, c_recv, g_send, g_recv, l_send, l_recv, r_send, r_recv, load,
+    c_send, c_recv, g_send, g_recv, l_send, l_recv, r_send, r_recv, load, done,
 ):
     width = prev_ref.shape[1]
     x_lanes = range(0, width - Y_FIRST * LANE, LANE)
@@ -363,9 +365,16 @@
                 scr[t, k, pl.ds(half * HALF, HALF), pl.ds(lane, LANE)] = jnp.concatenate(
                     kept, axis=0
                 ).astype(BF16)
+        for h in range(HI):
+            store(t, h).start()
         c_copy(t, k, 0, partner).start()
         c_copy(t, k, 1, right).start()
         c_copy(t, k, 2, left).start()
+
+    def store(t, h):
+        deep = CORE * 8
+        rows = pl.ds(pl.multiple_of((h * Z + chunk_z(t)) * deep, deep), deep)
+        return pltpu.make_async_copy(out_ref.at[rows], out_hbm.at[rows], done.at[t, h])
 
     def await_block(t, block):
         c_copy(t, block, 0, partner).wait_recv()
@@ -412,29 +421,15 @@
     depth = wide.shape[0] // 8
     wide_rows = wide.reshape(depth, 8, LANE)
 
-    def spread_block(n, carry):
-        at_row = pl.multiple_of(n * depth, depth)
+    def spread_block(n):
+        at_row = n * depth
         for lane in range(0, virtual, LANE):
             wide_rows[:, pl.ds(0, pairs_in), :] = x3_ref[pl.ds(at_row, depth), :, pl.ds(lane, LANE)].astype(F32)
             for i in range(pairs_in):
                 x_ref[pl.ds(at_row, depth), pl.ds(i * virtual + lane, LANE)] = wide[
                     pl.ds(i, depth, stride=8), :
                 ].astype(BF16)
-        return carry
-
-    lax.fori_loop(0, x3_ref.shape[0] // depth, spread_block, 0)
-    groups = []
-    for kk in range(LO * YS):
-        spot = lax.broadcasted_iota(jnp.int32, (per_sub, LANE), 0)
-        rows = jnp.zeros((per_sub, LANE), jnp.int32)
-        for s in range(per_sub):
-            rows = jnp.where(spot == s, local_rows[kk * per_sub + s], rows)
-        groups.append(rows)
-    rows = jnp.concatenate(groups, axis=0)
-    place = lax.broadcasted_iota(jnp.int32, (picks, LANE), 1)
-    chosen = jnp.concatenate(
-        [jnp.where(place + lane == rows, 1.0, 0.0) for lane in range(0, x_ref.shape[0], LANE)], axis=1
-    ).astype(BF16)
+
     acc[...] = jnp.zeros_like(acc)
 
     def to_diagonal():
@@ -443,25 +438,31 @@
     def relay_on():
         return remote(relayed, slab.at[z, core, 1 - hi], d_opp.at[0], d_recv.at[z, 1 - hi], partner)
 
+    states, orbitals = s3_ref.shape[1:]
+    assert states == 8
+
     def prepare_states(t):
-        states, orbitals = s3_ref.shape[1:]
-        assert states == 8
         s3_copy.wait()
-
-        def spread_states(n, carry):
-            at_row = pl.multiple_of(n * depth, depth)
+        for j, row in enumerate(local_rows):
+            raw = s3_ref[row].astype(F32)
             for lane in range(0, orbitals, LANE):
-                raw = s3_ref[pl.ds(at_row, depth), :, pl.ds(lane, LANE)].astype(F32)
-                wide[...] = raw.reshape(depth * states, LANE)
-                for state in range(states):
-                    s_ref[pl.ds(at_row, depth), pl.ds(state * orbitals + lane, LANE)] = wide[
-                        pl.ds(state, depth, stride=states), :
-                    ].astype(BF16)
-            return carry
-
-        lax.fori_loop(0, s3_ref.shape[0] // depth, spread_states, 0)
-        slab[z, core, hi] = jnp.dot(chosen, s_ref[...], preferred_element_type=F32).astype(BF16)
+                few[lane // LANE, j] = raw[:, lane : lane + LANE]
+        for state in range(states):
+            for lane in range(0, orbitals, LANE):
+                slab[z, core, hi, :, pl.ds(state * orbitals + lane, LANE)] = few_rows[
+                    lane // LANE, pl.ds(state, picks, stride=8), :
+                ].astype(BF16)
         start(to_diagonal())
+
+    def spread_states(n):
+        at_row = n * depth
+        for lane in range(0, orbitals, LANE):
+            raw = s3_ref[pl.ds(at_row, depth), :, pl.ds(lane, LANE)].astype(F32)
+            wide[...] = raw.reshape(depth * states, LANE)
+            for state in range(states):
+                s_ref[pl.ds(at_row, depth), pl.ds(state * orbitals + lane, LANE)] = wide[
+                    pl.ds(state, depth, stride=states), :
+                ].astype(BF16)
 
     def relay(t):
         to_diagonal().wait_recv()
@@ -488,6 +489,8 @@
         D_RING: lambda t: ring(d_set, t, 0, start, True),
         D_RING2: lambda t: ring(d_set, t, 1, start, True),
         D_PREP: prepare_states,
+        X_SPREAD: spread_block,
+        S_SPREAD: spread_states,
         PART_Y: part_y,
         PART_X: part_x,
         SUM: pair_sum,
@@ -506,7 +509,6 @@
 
     pairs = jnp.sum(acc[...], axis=0, keepdims=True)
     mine = hi * CORE + core
-    orbitals = orb_ref.shape[1]
     for n in range(state_idx.shape[0]):
         gap = mo_ref[state_idx[n]] - orb_ref[...]
         factor = gap / (gap * gap + 0.25)
@@ -524,6 +526,34 @@
     ]
     for n, (target, slot) in enumerate(chip):
         chip_copy(n, target).start()
+    finish(to_opposite(a_set))
+    finish(to_diagonal())
+    finish(relay_on())
+    for group in (a_set, d_set):
+        for h in range(HI):
+            finish(to_line(group, z, h, 0))
+            finish(to_line(group, z, h, 1))
+            finish(to_sibling(group, z, h))
+
+        for c in range(1, CHUNKS):
+            ring(group, c, 0, finish, False)
+            ring(group, c, 1, finish, False)
+
+    def drain(t, carry):
+        x_copy(t).wait_send()
+        for way in range(2):
+            y_copy(t, way).wait_send()
+            m_copy(t, way).wait_send()
+            n_copy(t, way).wait_send()
+            p_copy(t, way).wait_send()
+        w_copy(t).wait_send()
+        for h in range(HI):
+            store(t, h).wait()
+        for lane in range(7):
+            c_copy(t, k, lane, partner).wait_send()
+        return carry
+
+    lax.fori_loop(0, CHUNKS // 2, drain, 0)
     for n, (target, slot) in enumerate(chip):
         spot = sg_chip.at[slot]
         remote(spot, spot, g_send.at[n], g_recv.at[slot], target).wait_recv()
@@ -535,6 +565,7 @@
 
     for n, target in enumerate(line):
         line_copy(n, target).start()
+    lax.fori_loop(CHUNKS // 2, CHUNKS, drain, 0)
     for n, target in enumerate(line):
         slot = lax.rem(z + 1 + n, Z)
         spot = sg_line.at[slot]
@@ -549,32 +580,11 @@
         chip_copy(n, target).wait_send()
     for n, target in enumerate(line):
         line_copy(n, target).wait_send()
-    finish(to_opposite(a_set))
-    finish(to_diagonal())
-    finish(relay_on())
-    for group in (a_set, d_set):
-        for h in range(HI):
-            finish(to_line(group, z, h, 0))
-            finish(to_line(group, z, h, 1))
-            finish(to_sibling(group, z, h))
-
-        for c in range(1, CHUNKS):
-            ring(group, c, 0, finish, False)
-            ring(group, c, 1, finish, False)
-
-    def drain(t, carry):
-        x_copy(t).wait_send()
-        for way in range(2):
-            y_copy(t, way).wait_send()
-            m_copy(t, way).wait_send()
-            n_copy(t, way).wait_send()
-            p_copy(t, way).wait_send()
-        w_copy(t).wait_send()
-        for lane in range(7):
-            c_copy(t, k, lane, partner).wait_send()
-        return carry
-
-    lax.fori_loop(0, CHUNKS, drain, 0)
+
+
+def hand_over(panel_in, sig_in, panel_out, sig_out):
+    panel_out[...] = panel_in[...]
+    sig_out[...] = sig_in[...]
 
 
 def local(
@@ -615,7 +625,7 @@
             jax.ShapeDtypeStruct((1, ns_dev), F32),
         ),
         in_specs=[vmem, hbm, hbm, vmem, vmem] + [smem] * 4,
-        out_specs=(vmem, vmem),
+        out_specs=(hbm, vmem),
         scratch_shapes=[
             pltpu.VMEM((Z, CORE, HI, picks, pairs), BF16),
             pltpu.VMEM((Z, CORE, HI, picks, spread), BF16),
@@ -637,6 +647,7 @@
             pltpu.VMEM((col_block, p_dev), F32),
             pltpu.VMEM((p_dev, pairs), BF16),
             pltpu.VMEM((three_index.shape[2] // LANE, picks, 8, LANE), F32),
+            pltpu.VMEM((col_block, p_dev), F32),
             *ring_sems,
             *ring_sems,
             dma((CHUNKS,)), dma((CHUNKS,)),
@@ -648,7 +659,7 @@
             dma((CHUNKS, 7)), dma((CHUNKS, occ_count)),
             dma((3,)), dma((HI * CORE,)),
             dma((Z - 1,)), dma((Z,)),
-            dma((1,)), dma((1,)), dma((2,)),
+            dma((1,)), dma((1,)), dma((2,)), dma((CHUNKS, HI)),
         ],
         compiler_params=pltpu.CompilerParams(
             collective_id=0, has_side_effects=True, vmem_limit_bytes=60 * 2**20
@@ -661,6 +672,15 @@
         vir_energy.reshape(1, -1), orbital_energy.reshape(1, -1),
         mo_energy, occ_index, state_index, slab_rows,
     )
+    panel_out, sig = pl.pallas_call(
+        hand_over,
+        out_shape=(
+            jax.ShapeDtypeStruct((col_block, p_dev), F32),
+            jax.ShapeDtypeStruct((1, ns_dev), F32),
+        ),
+        in_specs=[vmem, vmem],
+        out_specs=(vmem, vmem),
+    )(panel_out, sig)
     return (panel_out, sig.reshape(ns_dev))
 
 

time: 113 us -> 111 us (0.982)
  local copies, waits for them, and re-layouts: 3.42 us -> 0 us
  Pallas kernels: 108 us -> 110 us
    unnamed x2 -> x0, local copies, waits for them, and re-layouts: 3.42 us -> none
    pallas_call x0 -> x1, Pallas kernels: none -> 2.27 us  [local(): pl.pallas_call(hand_over, out_shape=(jax.ShapeDtypeStruct((col_block, p_d...]
where the time goes in v4:
time: 111 us
  Pallas kernels  110 us (99%)
    pallas_call x1, Pallas kernels, local(): pl.pallas_call(kernel, out_shape=(jax.ShapeDtypeStruct((col_block, p_dev)...  108 us
    pallas_call x1, Pallas kernels, local(): pl.pallas_call(hand_over, out_shape=(jax.ShapeDtypeStruct((col_block, p_d...  2.27 us

profile of v4, /device:TPU:1, one launch (start us, length us, event | category | flops | bytes accessed | tf_op | source)
XLA Modules:
  0.0 111.1 jit_solution(2258742766652555976)
XLA Ops:
  0.6 108.2 %shard_map.104 = (f32[256,1024]{1,0:T(8,128)}, f32[1,8]{1,0:T(1,128)}) custom-call(bf16[1024,4,256]{2,1,0:T(4,128)(2,1)} %x3_ref.1, bf16[1024,8,256]{2,1,0:T(8,128)(2,1)} %s3_hbm.1, f32[256,1024]{1,0:T(8,128)} %prev_hbm.1, f32[1,256]{1,0:T(1,128)} %bitcast.3, f32[1,256]{1,0:T(1,128)} %bitcast.4, f32[1024]{0:T(1024)} %mo_ref.1, s32[4]{0:T(128)} %occ_idx.1, ...), custom_call_target="tpu_custom_call" | custom-call | flops 12999999488 | bytes 9437184 | tf_op jit(solution)/shard_map/pallas_call | solution.py:621
  108.9 2.3 %shard_map.105 = (f32[256,1024]{1,0:T(8,128)}, f32[1,8]{1,0:T(1,128)}) custom-call(f32[256,1024]{1,0:T(8,128)} %get-tuple-element.6.panel_in, f32[1,8]{1,0:T(1,128)} %get-tuple-element.7.sig_in), custom_call_target="tpu_custom_call" | custom-call | tf_op jit(solution)/shard_map/pallas_call | solution.py:675

commit v5 on v4

--- a/solution.py
+++ b/solution.py
@@ -9,6 +9,7 @@
 CHUNKS = Z
 LANE = 128
 HALF = 16
+VIA_X = (0, 1, 2, 3)
 Y_FIRST = 4
 
 (
@@ -16,27 +17,28 @@
     SUM_Y, PANEL, NEAR, FAR_R, FAR_L, PAIRS, X_SPREAD, S_SPREAD,
 ) = range(22)
 ORDER = (
-    (X_SPREAD, 4), (X_SPREAD, 5), (X_SPREAD, 6), (X_SPREAD, 7), (X_SPREAD, 0), (X_SPREAD, 1), (X_SPREAD, 2),
-    (X_SPREAD, 3), (D_PREP, 0), (A_RING, 1), (A_RING, 2), (A_OPP, 0), (S_SPREAD, 0), (S_SPREAD, 1),
-    (S_SPREAD, 2), (PART_Y, 0), (PART_X, 0), (S_SPREAD, 3), (S_SPREAD, 4), (PASS_Y, 0), (RELAY, 0),
-    (A_RING2, 1), (A_RING2, 2), (A_RING, 3), (A_RING, 4), (S_SPREAD, 5), (S_SPREAD, 6), (SUM, 0), (SUM_Y, 0),
-    (PART_Y, 1), (PART_Y, 2), (PART_X, 1), (PASS, 0), (PART_X, 2), (S_SPREAD, 7), (A_RING2, 3), (A_RING2, 4),
-    (A_RING, 5), (A_RING, 6), (D_OWN, 0), (PASS_Y, 1), (PANEL, 0), (PASS_Y, 2), (PART_Y, 3), (PART_Y, 4),
-    (D_OPP, 0), (PART_X, 3), (FAR_R, 0), (PART_X, 4), (SUM_Y, 1), (SUM_Y, 2), (NEAR, 0), (A_RING2, 6),
-    (PASS_Y, 3), (SUM, 1), (PASS_Y, 4), (FAR_L, 0), (A_RING2, 5), (SUM, 2), (A_RING, 7), (PART_Y, 5),
-    (PART_Y, 6), (PASS, 1), (PART_X, 5), (PASS, 2), (PART_X, 6), (D_RING, 2), (SUM, 3), (SUM, 4), (D_RING, 1),
-    (A_RING2, 7), (SUM_Y, 3), (PANEL, 1), (SUM_Y, 4), (PAIRS, 0, 0), (PASS_Y, 5), (D_RING2, 1), (PANEL, 2),
-    (PAIRS, 0, 1), (PART_Y, 7), (D_RING2, 2), (PART_X, 7), (PASS, 3), (PASS_Y, 6), (PAIRS, 0, 2), (PASS, 4),
-    (PAIRS, 0, 3), (SUM_Y, 5), (PANEL, 3), (FAR_R, 1), (SUM, 5), (PANEL, 4), (FAR_R, 2), (SUM_Y, 6),
-    (D_RING, 4), (NEAR, 1), (PASS_Y, 7), (NEAR, 2), (D_RING, 3), (D_RING2, 3), (SUM, 6), (D_RING2, 4),
-    (PASS, 5), (NEAR, 3), (NEAR, 4), (SUM, 7), (FAR_L, 1), (SUM_Y, 7), (FAR_R, 3), (FAR_L, 2), (D_RING, 6),
-    (PANEL, 5), (FAR_R, 4), (D_RING, 5), (PASS, 6), (FAR_L, 3), (D_RING2, 6), (D_RING2, 5), (NEAR, 5),
-    (FAR_L, 4), (PASS, 7), (PAIRS, 1, 0), (PAIRS, 1, 1), (PAIRS, 1, 2), (PAIRS, 1, 3), (PANEL, 6),
-    (PAIRS, 2, 0), (PAIRS, 2, 1), (PAIRS, 2, 2), (PAIRS, 2, 3), (PANEL, 7), (D_RING, 7), (NEAR, 6),
-    (D_RING2, 7), (FAR_R, 5), (PAIRS, 3, 0), (FAR_L, 5), (NEAR, 7), (PAIRS, 3, 1), (PAIRS, 3, 2),
-    (PAIRS, 3, 3), (PAIRS, 4, 0), (PAIRS, 4, 1), (PAIRS, 4, 2), (FAR_R, 6), (PAIRS, 4, 3), (FAR_L, 6),
-    (FAR_R, 7), (PAIRS, 5, 0), (FAR_L, 7), (PAIRS, 5, 1), (PAIRS, 5, 2), (PAIRS, 5, 3), (PAIRS, 6, 0),
-    (PAIRS, 6, 1), (PAIRS, 6, 2), (PAIRS, 6, 3), (PAIRS, 7, 0), (PAIRS, 7, 1), (PAIRS, 7, 2), (PAIRS, 7, 3),
+    (D_PREP, 0), (X_SPREAD, 4), (X_SPREAD, 5), (X_SPREAD, 6), (X_SPREAD, 7), (X_SPREAD, 0), (X_SPREAD, 1),
+    (A_RING, 1), (A_RING, 2), (X_SPREAD, 2), (X_SPREAD, 3), (A_OPP, 0), (S_SPREAD, 0), (S_SPREAD, 1),
+    (RELAY, 0), (PART_Y, 0), (PART_X, 0), (S_SPREAD, 2), (A_RING, 3), (A_RING, 4), (S_SPREAD, 3),
+    (A_RING2, 1), (A_RING2, 2), (PASS_Y, 0), (S_SPREAD, 4), (S_SPREAD, 5), (PART_Y, 1), (PART_Y, 2),
+    (PART_X, 1), (PART_X, 2), (SUM, 0), (A_RING, 5), (A_RING2, 3), (A_RING2, 4), (A_RING, 6), (SUM_Y, 0),
+    (S_SPREAD, 6), (PASS_Y, 1), (S_SPREAD, 7), (PASS, 0), (PASS_Y, 2), (PART_Y, 3), (PART_Y, 4), (D_OWN, 0),
+    (PART_X, 3), (PANEL, 0), (PART_X, 4), (SUM, 1), (A_RING2, 6), (SUM, 2), (A_RING2, 5), (A_RING, 7),
+    (SUM_Y, 1), (SUM_Y, 2), (D_OPP, 0), (PASS_Y, 3), (PART_Y, 5), (PART_Y, 6), (PART_X, 5), (PASS, 1),
+    (NEAR, 0), (PASS, 2), (PART_X, 6), (SUM_Y, 3), (PASS_Y, 4), (D_RING, 1), (PANEL, 1), (A_RING2, 7),
+    (PANEL, 2), (SUM, 3), (PASS_Y, 5), (D_RING, 2), (PASS_Y, 6), (PART_Y, 7), (PART_X, 7), (D_RING2, 1),
+    (SUM, 4), (SUM_Y, 4), (FAR_L, 0), (D_RING2, 2), (PASS, 3), (SUM_Y, 5), (SUM_Y, 6), (NEAR, 1), (FAR_R, 1),
+    (NEAR, 2), (D_RING, 3), (PASS, 4), (SUM, 5), (PANEL, 3), (PASS_Y, 7), (D_RING, 4), (SUM, 6), (FAR_R, 0),
+    (PANEL, 4), (D_RING2, 3), (SUM, 7), (D_RING2, 4), (NEAR, 3), (FAR_L, 1), (PASS, 5), (FAR_L, 2),
+    (PAIRS, 0, 0), (PAIRS, 0, 1), (NEAR, 4), (PAIRS, 0, 2), (SUM_Y, 7), (PAIRS, 0, 3), (PASS, 6),
+    (PAIRS, 1, 0), (PAIRS, 1, 1), (PAIRS, 1, 2), (PAIRS, 1, 3), (FAR_R, 3), (D_RING, 5), (PANEL, 5),
+    (PASS, 7), (FAR_R, 4), (D_RING, 6), (PANEL, 6), (NEAR, 5), (D_RING2, 5), (D_RING2, 6), (PANEL, 7),
+    (NEAR, 6), (FAR_R, 2), (FAR_L, 4), (D_RING, 7), (NEAR, 7), (FAR_L, 3), (PAIRS, 2, 0), (PAIRS, 2, 1),
+    (PAIRS, 2, 2), (FAR_R, 5), (PAIRS, 2, 3), (D_RING2, 7), (PAIRS, 3, 0), (FAR_L, 5), (PAIRS, 3, 1),
+    (FAR_R, 6), (PAIRS, 3, 2), (PAIRS, 3, 3), (FAR_L, 6), (PAIRS, 4, 0), (PAIRS, 4, 1), (FAR_R, 7),
+    (PAIRS, 4, 2), (FAR_L, 7), (PAIRS, 4, 3), (PAIRS, 5, 0), (PAIRS, 5, 1), (PAIRS, 5, 2), (PAIRS, 5, 3),
+    (PAIRS, 6, 0), (PAIRS, 6, 1), (PAIRS, 6, 2), (PAIRS, 6, 3), (PAIRS, 7, 0), (PAIRS, 7, 1), (PAIRS, 7, 2),
+    (PAIRS, 7, 3),
 )
 
 MESH = pl.DeviceIdType.MESH
@@ -88,10 +90,10 @@
 
 
 def kernel(
-    x3_ref, s3_hbm, prev_hbm, vir_ref, orb_ref, mo_ref, occ_idx, state_idx, slab_rows,
+    x3_hbm, s3_hbm, prev_hbm, vir_ref, orb_ref, mo_ref, occ_idx, state_idx, slab_rows,
     out_hbm, sig_ref,
     cols, slab, part, x_out, x_in, y_out, y_in, m_out, m_in, n_out, n_in, p_out, p_in, w_out, w_in,
-    scr, acc, sg_chip, sg_line, s_ref, wide, relayed, s3_ref, prev_ref, x_ref, few, out_ref,
+    scr, acc, sg_chip, sg_line, s_ref, wide, relayed, s3_ref, prev_ref, x_ref, few, out_ref, x3_ref,
     a_recv, a_sib, a_send, a_opp, d_recv, d_sib, d_send, d_opp,
     x_send, x_recv, y_send, y_recv, m_send, m_recv, n_send, n_recv, p_send, p_recv, w_send, w_recv,
     c_send, c_recv, g_send, g_recv, l_send, l_recv, r_send, r_recv, load, done,
@@ -127,11 +129,14 @@
 
     s3_copy = pltpu.make_async_copy(s3_hbm, s3_ref, load.at[0])
     prev_copy = pltpu.make_async_copy(prev_hbm, prev_ref, load.at[1])
+    x3_copy = pltpu.make_async_copy(x3_hbm, x3_ref, load.at[2])
+    x3_copy.start()
     barrier = pltpu.get_barrier_semaphore()
     friends = [sibling, opposite, across, partner, diagonal, right, left] + line
     for friend in friends:
         pl.semaphore_signal(barrier, inc=1, device_id=friend, device_id_type=MESH)
 
+    x3_copy.wait()
     s3_copy.start()
     prev_copy.start()
 
@@ -386,19 +391,35 @@
         c_copy(t, block, 4, left).start()
 
     def spread_right(t):
-        block = occ_at(lo, y_last)
+        if t in VIA_X and t % 2 == 0:
+            block, target = occ_at(xo, y_far), partner
+        else:
+            block, target = occ_at(lo, y_last), right
         await_block(t, block)
-        c_copy(t, block, 5, right).start()
+        c_copy(t, block, 5, target).start()
 
     def spread_left(t):
-        block = occ_at(xo, y_next)
+        if t in VIA_X and t % 2 == 1:
+            block, target = occ_at(lo, y_far), partner
+        else:
+            block, target = occ_at(xo, y_next), left
         await_block(t, block)
-        c_copy(t, block, 6, left).start()
+        c_copy(t, block, 6, target).start()
+
+    def rest(t):
+        blocks = [occ_at(xo, y_last), occ_at(lo, y_next)]
+        if t in VIA_X and t % 2 == 0:
+            blocks += [occ_at(lo, y_last), occ_at(lo, y_far)]
+        elif t in VIA_X:
+            blocks += [occ_at(xo, y_next), occ_at(xo, y_far)]
+        else:
+            blocks += [occ_at(lo, y_far), occ_at(xo, y_far)]
+        return blocks
 
     def energy(t, quarter):
         zz = chunk_z(t)
         if quarter == 0:
-            for block in (occ_at(xo, y_last), occ_at(lo, y_next), occ_at(lo, y_far), occ_at(xo, y_far)):
+            for block in rest(t):
                 await_block(t, block)
             await_sibling(d_set, zz)
         lhs = scr[t].reshape(LO * YS * 2 * HALF, width)
@@ -624,7 +645,7 @@
             jax.ShapeDtypeStruct((col_block, p_dev), F32),
             jax.ShapeDtypeStruct((1, ns_dev), F32),
         ),
-        in_specs=[vmem, hbm, hbm, vmem, vmem] + [smem] * 4,
+        in_specs=[hbm, hbm, hbm, vmem, vmem] + [smem] * 4,
         out_specs=(hbm, vmem),
         scratch_shapes=[
             pltpu.VMEM((Z, CORE, HI, picks, pairs), BF16),
@@ -648,6 +669,7 @@
             pltpu.VMEM((p_dev, pairs), BF16),
             pltpu.VMEM((three_index.shape[2] // LANE, picks, 8, LANE), F32),
             pltpu.VMEM((col_block, p_dev), F32),
+            pltpu.VMEM(three_index.shape, BF16),
             *ring_sems,
             *ring_sems,
             dma((CHUNKS,)), dma((CHUNKS,)),
@@ -659,7 +681,7 @@
             dma((CHUNKS, 7)), dma((CHUNKS, occ_count)),
             dma((3,)), dma((HI * CORE,)),
             dma((Z - 1,)), dma((Z,)),
-            dma((1,)), dma((1,)), dma((2,)), dma((CHUNKS, HI)),
+            dma((1,)), dma((1,)), dma((3,)), dma((CHUNKS, HI)),
         ],
         compiler_params=pltpu.CompilerParams(
             collective_id=0, has_side_effects=True, vmem_limit_bytes=60 * 2**20

time: 111 us -> 109 us (0.982)
  Pallas kernels: 110 us -> 108 us
    pallas_call x1, Pallas kernels: 108 us -> 106 us  [local(): pl.pallas_call(kernel, out_shape=(jax.ShapeDtypeStruct((col_block, p_dev)...]
where the time goes in v5:
time: 109 us
  Pallas kernels  108 us (99%)
    pallas_call x1, Pallas kernels, local(): pl.pallas_call(kernel, out_shape=(jax.ShapeDtypeStruct((col_block, p_dev)...  106 us
    pallas_call x1, Pallas kernels, local(): pl.pallas_call(hand_over, out_shape=(jax.ShapeDtypeStruct((col_block, p_d...  2.27 us

profile of v5, /device:TPU:1, one launch (start us, length us, event | category | flops | bytes accessed | tf_op | source)
XLA Modules:
  0.0 109.0 jit_solution(12985558020067497249)
XLA Ops:
  0.6 106.1 %shard_map.104 = (f32[256,1024]{1,0:T(8,128)}, f32[1,8]{1,0:T(1,128)}) custom-call(bf16[1024,4,256]{2,1,0:T(4,128)(2,1)} %x3_hbm.1, bf16[1024,8,256]{2,1,0:T(8,128)(2,1)} %s3_hbm.1, f32[256,1024]{1,0:T(8,128)} %prev_hbm.1, f32[1,256]{1,0:T(1,128)} %bitcast.3, f32[1,256]{1,0:T(1,128)} %bitcast.4, f32[1024]{0:T(1024)} %mo_ref.1, s32[4]{0:T(128)} %occ_idx.1, ...), custom_call_target="tpu_custom_call" | custom-call | flops 12999999488 | bytes 9437184 | tf_op jit(solution)/shard_map/pallas_call | solution.py:642
  106.8 2.3 %shard_map.105 = (f32[256,1024]{1,0:T(8,128)}, f32[1,8]{1,0:T(1,128)}) custom-call(f32[256,1024]{1,0:T(8,128)} %get-tuple-element.6.panel_in, f32[1,8]{1,0:T(1,128)} %get-tuple-element.7.sig_in), custom_call_target="tpu_custom_call" | custom-call | tf_op jit(solution)/shard_map/pallas_call | solution.py:697

commit v6 on v5

--- a/solution.py
+++ b/solution.py
@@ -9,6 +9,7 @@
 CHUNKS = Z
 LANE = 128
 HALF = 16
+PIECES = 4
 VIA_X = (0, 1, 2, 3)
 Y_FIRST = 4
 
@@ -17,26 +18,26 @@
     SUM_Y, PANEL, NEAR, FAR_R, FAR_L, PAIRS, X_SPREAD, S_SPREAD,
 ) = range(22)
 ORDER = (
-    (D_PREP, 0), (X_SPREAD, 4), (X_SPREAD, 5), (X_SPREAD, 6), (X_SPREAD, 7), (X_SPREAD, 0), (X_SPREAD, 1),
-    (A_RING, 1), (A_RING, 2), (X_SPREAD, 2), (X_SPREAD, 3), (A_OPP, 0), (S_SPREAD, 0), (S_SPREAD, 1),
+    (D_PREP, 0), (X_SPREAD, 4), (S_SPREAD, 0), (X_SPREAD, 5), (X_SPREAD, 6), (X_SPREAD, 7), (X_SPREAD, 0),
+    (X_SPREAD, 1), (A_RING, 1), (A_RING, 2), (X_SPREAD, 2), (X_SPREAD, 3), (A_OPP, 0), (S_SPREAD, 1),
     (RELAY, 0), (PART_Y, 0), (PART_X, 0), (S_SPREAD, 2), (A_RING, 3), (A_RING, 4), (S_SPREAD, 3),
-    (A_RING2, 1), (A_RING2, 2), (PASS_Y, 0), (S_SPREAD, 4), (S_SPREAD, 5), (PART_Y, 1), (PART_Y, 2),
-    (PART_X, 1), (PART_X, 2), (SUM, 0), (A_RING, 5), (A_RING2, 3), (A_RING2, 4), (A_RING, 6), (SUM_Y, 0),
-    (S_SPREAD, 6), (PASS_Y, 1), (S_SPREAD, 7), (PASS, 0), (PASS_Y, 2), (PART_Y, 3), (PART_Y, 4), (D_OWN, 0),
-    (PART_X, 3), (PANEL, 0), (PART_X, 4), (SUM, 1), (A_RING2, 6), (SUM, 2), (A_RING2, 5), (A_RING, 7),
-    (SUM_Y, 1), (SUM_Y, 2), (D_OPP, 0), (PASS_Y, 3), (PART_Y, 5), (PART_Y, 6), (PART_X, 5), (PASS, 1),
-    (NEAR, 0), (PASS, 2), (PART_X, 6), (SUM_Y, 3), (PASS_Y, 4), (D_RING, 1), (PANEL, 1), (A_RING2, 7),
-    (PANEL, 2), (SUM, 3), (PASS_Y, 5), (D_RING, 2), (PASS_Y, 6), (PART_Y, 7), (PART_X, 7), (D_RING2, 1),
-    (SUM, 4), (SUM_Y, 4), (FAR_L, 0), (D_RING2, 2), (PASS, 3), (SUM_Y, 5), (SUM_Y, 6), (NEAR, 1), (FAR_R, 1),
-    (NEAR, 2), (D_RING, 3), (PASS, 4), (SUM, 5), (PANEL, 3), (PASS_Y, 7), (D_RING, 4), (SUM, 6), (FAR_R, 0),
-    (PANEL, 4), (D_RING2, 3), (SUM, 7), (D_RING2, 4), (NEAR, 3), (FAR_L, 1), (PASS, 5), (FAR_L, 2),
-    (PAIRS, 0, 0), (PAIRS, 0, 1), (NEAR, 4), (PAIRS, 0, 2), (SUM_Y, 7), (PAIRS, 0, 3), (PASS, 6),
-    (PAIRS, 1, 0), (PAIRS, 1, 1), (PAIRS, 1, 2), (PAIRS, 1, 3), (FAR_R, 3), (D_RING, 5), (PANEL, 5),
-    (PASS, 7), (FAR_R, 4), (D_RING, 6), (PANEL, 6), (NEAR, 5), (D_RING2, 5), (D_RING2, 6), (PANEL, 7),
-    (NEAR, 6), (FAR_R, 2), (FAR_L, 4), (D_RING, 7), (NEAR, 7), (FAR_L, 3), (PAIRS, 2, 0), (PAIRS, 2, 1),
-    (PAIRS, 2, 2), (FAR_R, 5), (PAIRS, 2, 3), (D_RING2, 7), (PAIRS, 3, 0), (FAR_L, 5), (PAIRS, 3, 1),
-    (FAR_R, 6), (PAIRS, 3, 2), (PAIRS, 3, 3), (FAR_L, 6), (PAIRS, 4, 0), (PAIRS, 4, 1), (FAR_R, 7),
-    (PAIRS, 4, 2), (FAR_L, 7), (PAIRS, 4, 3), (PAIRS, 5, 0), (PAIRS, 5, 1), (PAIRS, 5, 2), (PAIRS, 5, 3),
+    (A_RING2, 1), (A_RING2, 2), (PASS_Y, 0), (S_SPREAD, 4), (PART_Y, 1), (PART_Y, 2), (PART_X, 1),
+    (PART_X, 2), (SUM, 0), (A_RING, 5), (A_RING2, 4), (S_SPREAD, 5), (A_RING2, 3), (PASS_Y, 1), (PASS_Y, 2),
+    (SUM_Y, 0), (PASS, 0), (S_SPREAD, 6), (PART_Y, 3), (PART_Y, 4), (D_OWN, 0), (PART_X, 3), (PANEL, 0),
+    (A_RING, 6), (PART_X, 4), (A_RING2, 6), (SUM, 1), (SUM, 2), (A_RING2, 5), (S_SPREAD, 7), (PASS_Y, 3),
+    (D_OPP, 0), (SUM_Y, 1), (PART_Y, 5), (PART_Y, 6), (PART_X, 6), (PASS, 1), (A_RING, 7), (SUM_Y, 2),
+    (PASS_Y, 4), (NEAR, 0), (PART_X, 5), (PASS, 2), (D_RING, 1), (SUM_Y, 3), (PANEL, 1), (PANEL, 2),
+    (D_RING, 2), (A_RING2, 7), (SUM, 3), (PASS_Y, 5), (PASS_Y, 6), (PART_Y, 7), (SUM, 4), (SUM_Y, 4),
+    (FAR_L, 0), (D_RING2, 1), (PART_X, 7), (PASS, 3), (D_RING2, 2), (SUM_Y, 6), (NEAR, 1), (FAR_R, 1),
+    (PASS, 4), (NEAR, 2), (SUM_Y, 5), (SUM, 5), (D_RING, 3), (PANEL, 3), (FAR_R, 0), (PASS_Y, 7), (SUM, 6),
+    (D_RING, 4), (PANEL, 4), (D_RING2, 4), (D_RING2, 3), (SUM, 7), (FAR_L, 1), (NEAR, 3), (PASS, 5),
+    (PAIRS, 0, 0), (NEAR, 4), (PAIRS, 0, 1), (FAR_L, 2), (PASS, 6), (PAIRS, 0, 2), (SUM_Y, 7), (FAR_R, 3),
+    (PAIRS, 0, 3), (PAIRS, 1, 0), (PAIRS, 1, 1), (PAIRS, 1, 2), (D_RING, 5), (PAIRS, 1, 3), (PANEL, 5),
+    (PASS, 7), (FAR_R, 4), (D_RING, 6), (PANEL, 6), (D_RING2, 5), (NEAR, 5), (D_RING2, 6), (PANEL, 7),
+    (FAR_L, 4), (FAR_R, 2), (NEAR, 6), (FAR_L, 3), (NEAR, 7), (PAIRS, 2, 0), (D_RING, 7), (PAIRS, 2, 1),
+    (PAIRS, 2, 2), (FAR_R, 5), (FAR_L, 5), (PAIRS, 2, 3), (D_RING2, 7), (PAIRS, 3, 0), (PAIRS, 3, 1),
+    (PAIRS, 3, 2), (PAIRS, 3, 3), (FAR_R, 6), (FAR_L, 6), (PAIRS, 4, 0), (PAIRS, 4, 1), (PAIRS, 4, 2),
+    (PAIRS, 4, 3), (FAR_R, 7), (FAR_L, 7), (PAIRS, 5, 0), (PAIRS, 5, 1), (PAIRS, 5, 2), (PAIRS, 5, 3),
     (PAIRS, 6, 0), (PAIRS, 6, 1), (PAIRS, 6, 2), (PAIRS, 6, 3), (PAIRS, 7, 0), (PAIRS, 7, 1), (PAIRS, 7, 2),
     (PAIRS, 7, 3),
 )
@@ -603,9 +604,20 @@
         line_copy(n, target).wait_send()
 
 
-def hand_over(panel_in, sig_in, panel_out, sig_out):
-    panel_out[...] = panel_in[...]
+def hand_over(panel_in, sig_in, panel_out, sig_out, held, in_sems, out_sems):
+    deep = panel_in.shape[0] // PIECES
+    loads, stores = [], []
+    for n in range(PIECES):
+        rows = pl.ds(n * deep, deep)
+        loads.append(pltpu.make_async_copy(panel_in.at[rows], held.at[rows], in_sems.at[n]))
+        stores.append(pltpu.make_async_copy(held.at[rows], panel_out.at[rows], out_sems.at[n]))
+        loads[n].start()
     sig_out[...] = sig_in[...]
+    for n in range(PIECES):
+        loads[n].wait()
+        stores[n].start()
+    for copy in stores:
+        copy.wait()
 
 
 def local(
@@ -700,8 +712,9 @@
             jax.ShapeDtypeStruct((col_block, p_dev), F32),
             jax.ShapeDtypeStruct((1, ns_dev), F32),
         ),
-        in_specs=[vmem, vmem],
-        out_specs=(vmem, vmem),
+        in_specs=[hbm, vmem],
+        out_specs=(hbm, vmem),
+        scratch_shapes=[pltpu.VMEM((col_block, p_dev), F32), dma((PIECES,)), dma((PIECES,))],
     )(panel_out, sig)
     return (panel_out, sig.reshape(ns_dev))
 

time: 109 us -> 109 us (level)
  no operation moved by 1% of the time
where the time goes in v6:
time: 109 us
  Pallas kernels  108 us (99%)
    pallas_call x1, Pallas kernels, local(): pl.pallas_call(kernel, out_shape=(jax.ShapeDtypeStruct((col_block, p_dev)...  105 us
    pallas_call x1, Pallas kernels, local(): pl.pallas_call(hand_over, out_shape=(jax.ShapeDtypeStruct((col_block, p_d...  3.12 us

profile of v6, /device:TPU:1, one launch (start us, length us, event | category | flops | bytes accessed | tf_op | source)
XLA Modules:
  0.0 109.2 jit_solution(4389813330973294061)
XLA Ops:
  0.6 105.2 %shard_map.104 = (f32[256,1024]{1,0:T(8,128)}, f32[1,8]{1,0:T(1,128)}) custom-call(bf16[1024,4,256]{2,1,0:T(4,128)(2,1)} %x3_hbm.1, bf16[1024,8,256]{2,1,0:T(8,128)(2,1)} %s3_hbm.1, f32[256,1024]{1,0:T(8,128)} %prev_hbm.1, f32[1,256]{1,0:T(1,128)} %bitcast.3, f32[1,256]{1,0:T(1,128)} %bitcast.4, f32[1024]{0:T(1024)} %mo_ref.1, s32[4]{0:T(128)} %occ_idx.1, ...), custom_call_target="tpu_custom_call" | custom-call | flops 12999999488 | bytes 9437184 | tf_op jit(solution)/shard_map/pallas_call | solution.py:654
  105.9 3.1 %shard_map.105 = (f32[256,1024]{1,0:T(8,128)}, f32[1,8]{1,0:T(1,128)}) custom-call(f32[256,1024]{1,0:T(8,128)} %get-tuple-element.6.panel_in, f32[1,8]{1,0:T(1,128)} %get-tuple-element.7.sig_in), custom_call_target="tpu_custom_call" | custom-call | tf_op jit(solution)/shard_map/pallas_call | solution.py:709
